TPU v7x, 256 devices: a whole 4x4x8 slice. The times are simulated.
256 devices in a mesh: row: 8 (over x, z_hi), samp: 32 (over y, z_lo, core).
Axes of the slice: x: 4, y: 4, z: 8 (z_hi: 2, z_lo: 4; z = z_hi * 4 + z_lo), core: 2. Of those that a mesh axis runs over, the one named last changes fastest.
Arguments:
- activations: bfloat16 [32, 1024, 768], P('samp', 'row'), may hold values from -6 to 6
- pair_bias: bfloat16 [16, 1024, 1024], P(None, ('row', 'samp')), may hold values from -10 to 240
- w_qkv: bfloat16 [768, 2304], replicated, may hold values from -0.21875 to 0.21875
- w_out: bfloat16 [768, 768], replicated, may hold values from -0.21875 to 0.21875
- cotangent: bfloat16 [32, 1024, 768], P('samp', 'row'), may hold values from -6 to 6
Outputs:
- update: bfloat16 [32, 1024, 768], P('samp', 'row')
- grad_act: bfloat16 [32, 1024, 768], P('samp', 'row')
- grad_pair: bfloat16 [16, 1024, 1024], P(None, ('row', 'samp'))
- grad_weights: float32 [768, 3072], P(('row', 'samp'))
All inputs are finite; a program needn't handle non-finite values.
Results may differ from a plain program's by a relative error of at most 0.025.
Values may be sent and summed in bfloat16 or wider, within the bound.
No kernel may reach another device: no remote copies, remote signals or barrier semaphores. Data moves between devices by JAX's collectives and lax.ppermute only.
A program may use at most 128 MiB of HBM per device.

v0:
```python
import math

import jax
import jax.numpy as jnp
from jax import lax
from jax.experimental import pallas as pl
from jax.experimental.pallas import tpu as pltpu
from jax.sharding import Mesh, PartitionSpec as P

H = 16
HEAD = 48
PAD = 128
AXES = ("x", "zh", "y", "zl", "c")
VMEM_LIMIT = 56 * 1024 * 1024

epsilon = 1e-05
F32 = jnp.float32
BF16 = jnp.bfloat16


def layer_norm(values):
    mean_value = jnp.mean(values, axis=-1, keepdims=True)
    centred = values - mean_value
    variance = jnp.mean(centred * centred, axis=-1, keepdims=True)
    inverse = lax.rsqrt(variance + epsilon)
    return (centred * inverse, inverse)


def norm_backward(grad_in, normed, inverse):
    first_mean = jnp.mean(grad_in, axis=-1, keepdims=True)
    second_mean = jnp.mean(grad_in * normed, axis=-1, keepdims=True)
    return inverse * (grad_in - first_mean - normed * second_mean)


def right_transposed(left, right):
    return lax.dot_general(left, right, (((1,), (1,)), ((), ())), preferred_element_type=F32)


def normalise(values):
    mean_value = jnp.mean(values, axis=-1, keepdims=True)
    centred = values - mean_value
    variance = jnp.mean(centred * centred, axis=-1, keepdims=True)
    return (centred * lax.rsqrt(variance + epsilon)).astype(BF16)


def cost(us):
    return pl.CostEstimate(flops=int(us * 1e9), bytes_accessed=int(us * 3e6), transcendentals=0)


def select_heads(window, offset):
    source = lax.broadcasted_iota(jnp.int32, (window.shape[1], PAD), 0)
    target = lax.broadcasted_iota(jnp.int32, (window.shape[1], PAD), 1)
    chosen = ((source == offset + target) & (target < 2 * HEAD)).astype(F32).astype(BF16)
    return jnp.dot(window, chosen, preferred_element_type=F32).astype(BF16)


def columns_kernel(place, w_qkv, w_out, columns, rows):
    width = w_out.shape[0]
    part = 2 * HEAD
    first = (place[0] * 2 + place[4]) * part
    start = jnp.minimum(lax.div(first, PAD) * PAD, width - 2 * PAD)
    for kind in range(3):
        lanes = pl.ds(pl.multiple_of(kind * width + start, PAD), 2 * PAD)
        columns[:, kind * PAD : (kind + 1) * PAD] = select_heads(w_qkv[:, lanes], first - start)
    own = w_out[pl.ds(pl.multiple_of(first, 16), part), :]
    rows[...] = jnp.concatenate([own, jnp.zeros((PAD - part, width), BF16)], axis=0).T


def own_columns(place, w_qkv, w_out):
    width = w_out.shape[0]
    whole = pl.BlockSpec(memory_space=pltpu.VMEM)
    return pl.pallas_call(
        columns_kernel,
        in_specs=[pl.BlockSpec(memory_space=pltpu.SMEM)] + [whole] * 2,
        out_specs=[whole] * 2,
        out_shape=[
            jax.ShapeDtypeStruct((width, 3 * PAD), BF16),
            jax.ShapeDtypeStruct((width, PAD), BF16),
        ],
        compiler_params=pltpu.CompilerParams(vmem_limit_bytes=VMEM_LIMIT),
        cost_estimate=cost(2),
        name="own_columns",
    )(place, w_qkv, w_out)


def project_kernel(number, *refs):
    pieces, twins, columns, rows = refs[:number], refs[number : 2 * number], refs[2 * number], refs[2 * number + 1]
    normed, outs = refs[-2 * number : -number], refs[-number:]
    count = pieces[0].shape[1]
    kinds = outs[0].shape[1] // (2 * HEAD)
    parts = [[], []]
    cots = []
    for i in range(number):
        for t, ref in enumerate((pieces[i], twins[i])):
            for part in range(2):
                value = normalise(ref[part].astype(F32))
                normed[i][t, part] = value
                parts[part].append(value)
            cots.append(ref[2])
    own = jnp.dot(jnp.concatenate(parts[0], axis=0), columns[...], preferred_element_type=F32)
    far = jnp.dot(jnp.concatenate(parts[1], axis=0), columns[:, PAD:], preferred_element_type=F32)
    grads = jnp.dot(jnp.concatenate(cots, axis=0), rows[...], preferred_element_type=F32)
    blocks = [own[:, :PAD], own[:, PAD : 2 * PAD], own[:, 2 * PAD :], grads, far[:, :PAD], far[:, PAD:]]
    for i in range(number):
        for t in range(2):
            for kind, block in enumerate(blocks):
                at = (2 * i + t) * count
                turned = block[at : at + count].T.astype(BF16)
                for h in range(2):
                    low = (h * kinds + kind) * HEAD
                    outs[i][t, low : low + HEAD] = turned[h * HEAD : (h + 1) * HEAD]


def project(pieces, twins, columns, rows):
    number = len(pieces)
    _, count, width = pieces[0].shape
    whole = pl.BlockSpec(memory_space=pltpu.VMEM)
    return pl.pallas_call(
        lambda *refs: project_kernel(number, *refs),
        in_specs=[whole] * (2 * number + 2),
        out_specs=[whole] * (2 * number),
        out_shape=[jax.ShapeDtypeStruct((2, 2, count, width), BF16)] * number
        + [jax.ShapeDtypeStruct((2, 12 * HEAD, count), BF16)] * number,
        compiler_params=pltpu.CompilerParams(vmem_limit_bytes=VMEM_LIMIT),
        cost_estimate=cost(2 * number),
        name="project",
    )(*pieces, *twins, columns, rows)


def gate(values, *after):
    away = pl.BlockSpec(memory_space=pl.ANY)
    return pl.pallas_call(
        lambda *refs: None,
        in_specs=[away] * (1 + len(after)),
        out_specs=away,
        out_shape=jax.ShapeDtypeStruct(values.shape, values.dtype),
        input_output_aliases={0: 0},
        cost_estimate=cost(0.1),
        name="gate",
    )(values, *after)


def weights_kernel(place, sent, *refs):
    outs, (turned, out_acc, piece) = refs[-7:-3], refs[-3:]
    at_x, at_zh, at_y, at_c = place[0], place[1], place[2], place[4]
    nx, _, heads, _, _ = sent.shape
    normed, cots = refs[:nx], refs[nx : 3 * nx]
    width = normed[0].shape[-1]
    ny = len(outs)
    sums = [None] * 3

    def stacked(x, s, slots):
        return jnp.concatenate(
            [
                sent[x, s, h, pl.ds(pl.multiple_of(slot * HEAD, 16), HEAD), :]
                for slot in slots
                for h in range(heads)
            ],
            axis=0,
        )

    order = [lax.rem(at_x + shift, nx) for shift in range(nx)]
    for twin in range(2):
        s = lax.rem(at_c + twin, 2)
        own, other = 2 + 2 * at_zh, 4 - 2 * at_zh
        kv_left = jnp.concatenate(
            [stacked(x, s, (own, own + 1)) for x in order]
            + [stacked(x, s, (other, other + 1)) for x in order],
            axis=1,
        )
        q_left = jnp.concatenate([stacked(x, s, (1,)) for x in order], axis=1)
        out_left = jnp.concatenate([stacked(x, s, (0,)) for x in order], axis=1)
        own_right = jnp.concatenate([p[twin, 0] for p in normed], axis=0)
        other_right = jnp.concatenate([p[twin, 1] for p in normed], axis=0)
        out_right = jnp.concatenate([p[0] for p in cots[twin * nx : (twin + 1) * nx]], axis=0)
        terms = (
            jnp.dot(q_left, own_right, preferred_element_type=F32),
            jnp.dot(kv_left, jnp.concatenate([own_right, other_right], axis=0), preferred_element_type=F32),
            jnp.dot(out_left, out_right, preferred_element_type=F32),
        )
        sums = [t if a is None else a + t for a, t in zip(sums, terms)]
    part = heads * HEAD
    blank = jnp.zeros((PAD - part, width), F32)
    for kind, block in enumerate((sums[0], sums[1][:part], sums[1][part:])):
        turned[:, kind * PAD : (kind + 1) * PAD] = jnp.concatenate([block, blank], axis=0).T
    out_acc[...] = sums[2]
    three = part // ny
    halfway = width // 2
    for shift in range(ny):
        low = lax.rem(at_y + shift, ny) * three
        count = width // part
        for j in range(count):
            piece[j * three : (j + 1) * three] = turned[pl.ds(pl.multiple_of(j * part + low, 8), three), :]
        for j in range(2):
            piece[(count + j) * three : (count + j + 1) * three] = out_acc[
                pl.ds(pl.multiple_of(low, 8), three), j * halfway : (j + 1) * halfway
            ]
        outs[shift][...] = piece[...].astype(BF16)


def weight_grads(place, sent, normed, pieces, ny, after):
    heads, rows = sent.shape[2], sent.shape[4]
    width = normed[0].shape[-1]
    part = heads * HEAD
    height = (width // part + 2) * (part // ny)
    whole = lambda a: pl.BlockSpec(a.shape, lambda i: (0,) * a.ndim)
    cot_spec = pl.BlockSpec((1, rows, width), lambda i: (2, 0, 0))
    out = jax.ShapeDtypeStruct((height, 3 * PAD), BF16)
    return pl.pallas_call(
        weights_kernel,
        grid=(1,),
        in_specs=[pl.BlockSpec(memory_space=pltpu.SMEM), whole(sent)]
        + [whole(v) for v in normed]
        + [cot_spec] * len(pieces)
        + [pl.BlockSpec(memory_space=pl.ANY)] * len(after),
        out_specs=[pl.BlockSpec(out.shape, lambda i: (0, 0))] * ny,
        out_shape=[out] * ny,
        scratch_shapes=[
            pltpu.VMEM((width, 3 * PAD), F32),
            pltpu.VMEM((part, width), F32),
            pltpu.VMEM((height, 3 * PAD), F32),
        ],
        compiler_params=pltpu.CompilerParams(vmem_limit_bytes=VMEM_LIMIT),
        cost_estimate=cost(6),
        name="weight_grads",
    )(place, sent, *normed, *pieces, *after)


def attention_kernel(scale, place, *refs):
    own_refs, bias_refs, send_ref, pair_refs = refs[:4], refs[4:8], refs[-15], refs[-14:-10]
    bias, pair, kt, vt, k_all, v_all, qt, gt, dk_acc, dv_acc = refs[-10:]
    step = pl.program_id(0)
    at_x, at_zh, at_y, at_c = place[0], place[1], place[2], place[4]
    nx = len(own_refs)
    rows = own_refs[0].shape[2]
    wide = bias.shape[0] // rows
    ny = len(bias_refs)
    chunk = rows // ny
    total = kt.shape[2]
    block = wide * rows
    spots = []
    for x in range(wide):
        for shift in range(ny):
            start = x * rows + lax.rem(at_y + shift, ny) * chunk
            spots.append((x, shift, pl.ds(pl.multiple_of(start, chunk), chunk)))

    @pl.when(step == 0)
    def _():
        for ref in (kt, vt, qt, gt, dk_acc, dv_acc):
            ref[...] = jnp.zeros_like(ref)
        for t in range(2):
            for shift in range(nx):
                slot = lax.rem(at_x + shift, nx)
                own = pl.ds(pl.multiple_of((slot * 2 + at_zh) * rows, rows), rows)
                other = pl.ds(pl.multiple_of((slot * 2 + 1 - at_zh) * rows, rows), rows)
                here = pl.ds(pl.multiple_of(slot * rows, rows), rows)
                for kind, (ref, lanes) in enumerate(
                    ((qt, here), (kt, own), (vt, own), (gt, here), (kt, other), (vt, other))
                ):
                    low = kind * HEAD
                    ref[t, :HEAD, lanes] = own_refs[shift][t, low : low + HEAD, :]
            k_all[t] = kt[t].T
            v_all[t] = vt[t].T

    for x, shift, spot in spots:
        bias[spot, :] = bias_refs[shift][x]
    lanes = pl.ds(pl.multiple_of(step * block, block), block)
    for t in range(2):
        s = lax.rem(at_c + t, 2)
        q_t, g_t = qt[t, :, lanes], gt[t, :, lanes]
        scores = jnp.dot(q_t.T, kt[t], preferred_element_type=F32) * scale + bias[...].astype(F32)
        peak = jnp.max(scores, axis=-1, keepdims=True)
        expo = jnp.exp(scores - peak)
        probs = expo * (1.0 / jnp.sum(expo, axis=-1, keepdims=True))
        probs_b = probs.astype(BF16)
        att = jnp.dot(probs_b, v_all[t], preferred_element_type=F32).T
        grad_prob = jnp.dot(g_t.T, vt[t], preferred_element_type=F32)
        centre = jnp.sum(probs * grad_prob, axis=-1, keepdims=True)
        grad_score = probs * (grad_prob - centre)
        score_b = grad_score.astype(BF16)
        if t == 0:
            pair[...] = grad_score
        else:
            pair[...] += grad_score
        dq = (jnp.dot(score_b, k_all[t], preferred_element_type=F32) * scale).T
        dk_acc[t] += jnp.dot(q_t, score_b, preferred_element_type=F32)
        dv_acc[t] += jnp.dot(g_t, probs_b, preferred_element_type=F32)
        for x in range(wide):
            send_ref[step * wide + x, s, 0, :HEAD] = att[:HEAD, x * rows : (x + 1) * rows].astype(BF16)
            send_ref[step * wide + x, s, 0, HEAD : 2 * HEAD] = dq[:HEAD, x * rows : (x + 1) * rows].astype(BF16)
    for x, shift, spot in spots:
        pair_refs[shift][x] = pair[spot, :].astype(BF16)

    @pl.when(step == pl.num_programs(0) - 1)
    def _():
        for t in range(2):
            s = lax.rem(at_c + t, 2)
            for at in range(total // rows):
                x, zh = at // 2, at % 2
                low = (2 + 2 * zh) * HEAD
                part = slice(at * rows, (at + 1) * rows)
                send_ref[x, s, 0, low : low + HEAD] = (dk_acc[t, :HEAD, part] * scale).astype(BF16)
                send_ref[x, s, 0, low + HEAD : low + 2 * HEAD] = dv_acc[t, :HEAD, part].astype(BF16)


def attention(head, heads, place, own, bias, sent, scale):
    nx, chunk, total = bias[0].shape
    rows = own[0].shape[2]
    wide = 2
    block = wide * rows
    own_spec = pl.BlockSpec((2, 6 * HEAD, rows), lambda i: (0, head, 0))
    bias_spec = pl.BlockSpec((wide, chunk, total), lambda i: (i, 0, 0))
    pair_shape = jax.ShapeDtypeStruct(bias[0].shape, BF16)
    return pl.pallas_call(
        lambda *refs: attention_kernel(scale, *refs),
        grid=(nx // wide,),
        in_specs=[pl.BlockSpec(memory_space=pltpu.SMEM)]
        + [own_spec] * 4
        + [bias_spec] * 4
        + [pl.BlockSpec(memory_space=pl.ANY)] * len(sent),
        out_specs=[pl.BlockSpec((nx, 2, 1, 6 * HEAD, rows), lambda i: (0, 0, head, 0, 0))] + [bias_spec] * 4,
        out_shape=[jax.ShapeDtypeStruct((nx, 2, heads, 6 * HEAD, rows), BF16)] + [pair_shape] * 4,
        input_output_aliases={9 + i: i for i in range(len(sent))},
        scratch_shapes=[
            pltpu.VMEM((block, total), BF16),
            pltpu.VMEM((block, total), F32),
            pltpu.VMEM((2, PAD, total), BF16),
            pltpu.VMEM((2, PAD, total), BF16),
            pltpu.VMEM((2, total, PAD), BF16),
            pltpu.VMEM((2, total, PAD), BF16),
            pltpu.VMEM((2, PAD, nx * rows), BF16),
            pltpu.VMEM((2, PAD, nx * rows), BF16),
            pltpu.VMEM((2, PAD, total), F32),
            pltpu.VMEM((2, PAD, total), F32),
        ],
        compiler_params=pltpu.CompilerParams(vmem_limit_bytes=VMEM_LIMIT),
        cost_estimate=cost(9),
        name="attention",
    )(place, *own, *bias, *sent)


def exchange(values, axes):
    return lax.all_to_all(values, axes, split_axis=0, concat_axis=0, tiled=True)


def ring(n, shift):
    return [(i, (i + shift) % n) for i in range(n)]


def around(values, axis):
    n = lax.axis_size(axis)
    return [values] + [lax.ppermute(values, axis, ring(n, -shift)) for shift in range(1, n)]


def ring_scatter(pieces, axis):
    n = lax.axis_size(axis)
    return [lax.ppermute(pieces[shift], axis, ring(n, shift)) for shift in range(1, n)]


def added(own, got):
    total = own.astype(F32)
    for piece in got:
        total = total + piece.astype(F32)
    return total


def per_device(activations, pair_bias, w_qkv, w_out, cotangent):
    act = activations[0]
    cot = cotangent[0]
    rows, width = act.shape
    nx, nzh, ny, nzl, nc = (lax.axis_size(a) for a in AXES)
    place = jnp.stack([lax.axis_index(a) for a in AXES]).astype(jnp.int32)
    at_x, at_zh, at_c = place[0], place[1], place[4]
    groups = nx * nc
    heads = H // groups
    part = width // groups
    scale = 1.0 / math.sqrt(HEAD)
    total = pair_bias.shape[2]
    own_rows = pair_bias.shape[1]
    chunk = nzl * nc * own_rows
    swap = [(0, 1), (1, 0)]

    with jax.named_scope("rows_in"):
        act_other = lax.ppermute(act, "zh", swap)
        columns, rows_out = own_columns(place, w_qkv, w_out)
        pieces = around(jnp.stack([act, act_other, cot]), "x")
        twin = lax.ppermute(pieces[0], "c", swap)

    with jax.named_scope("project"):
        first = project(pieces[:1], [twin], columns, rows_out)

    with jax.named_scope("bias_in"):
        send = pair_bias.reshape(nx, 1, nc, heads, own_rows, total)
        send = jnp.broadcast_to(send, (nx, nzl, nc, heads, own_rows, total))
        got = exchange(send.reshape(nx * nzl * nc, heads, own_rows, total), ("x", "zl", "c"))
        got = gate(got, first[1]).reshape(nx, nzl * nc, heads, own_rows, total)
        bias = [around(got[:, :, h].reshape(nx, chunk, total), "y") for h in range(heads)]

    with jax.named_scope("project"):
        ready = [first[1], bias[0][0], bias[1][0]]
        ready = [[], ready, bias[0][1:], ready]
        pieces = pieces[:1] + [gate(pieces[i], *ready[i]) for i in range(1, nx)]
        twins = [twin] + [lax.ppermute(piece, "c", swap) for piece in pieces[1:]]
        later = project(pieces[1:], twins[1:], columns, rows_out)
        normed = first[:1] + later[: nx - 1]
        own = first[1:] + later[nx - 1 :]

    sent = []
    pairs_out = []
    with jax.named_scope("attention"):
        for h in range(heads):
            out, *pair = attention(h, heads, place, own, bias[h], sent, scale)
            sent = [out]
            pairs_out.append(pair)

    with jax.named_scope("along_y"):
        arrived = [ring_scatter(pair, "y") for pair in pairs_out]
        sums = [added(pair[0], got) for pair, got in zip(pairs_out, arrived)]
        sums = [v.astype(BF16).reshape(nx * nzl * nc, own_rows, total) for v in sums]

    with jax.named_scope("weights"):
        weight_pieces = weight_grads(place, sent[0], normed, pieces + twins, ny, arrived[0][:1])

    with jax.named_scope("along_y"):
        weight_sum = added(weight_pieces[0], ring_scatter(weight_pieces, "y")).astype(BF16)

    with jax.named_scope("owners"):
        three = width // (nx * nzh * ny * nzl * nc)
        cut = nx * nzh * nzl * nc * three
        qkv_part = weight_sum[:cut].reshape(nx, nzh, nzl, nc, three, 3 * PAD).transpose(0, 2, 3, 1, 4, 5)
        out_part = weight_sum[cut:].reshape(1, 2, nzl, nc, three, width // 2).transpose(0, 2, 3, 1, 4, 5)
        here = (jnp.arange(nx) == at_x).reshape(nx, 1, 1, 1, 1, 1)
        out_part = jnp.where(here, out_part, jnp.zeros_like(out_part))
        peers = nx * nzl * nc
        weight_send = jnp.concatenate(
            [qkv_part.reshape(peers, -1), out_part.reshape(peers, -1)], axis=1
        ).reshape(peers, heads * own_rows, -1)
        pair_send = jnp.concatenate(sums, axis=1)
        got = exchange(jnp.concatenate([pair_send, weight_send], axis=2), ("x", "zl", "c"))
        pair_got = got[:, :, :total].reshape(nx, nzl, nc, heads, own_rows, total).astype(F32)
        grad_pair = jnp.sum(pair_got, axis=1).astype(BF16).reshape(H, own_rows, total)
        weight_got = jnp.sum(got[:, :, total:].reshape(nx, nzl, nc, -1).astype(F32), axis=1)
        cut = nzh * three * 3 * PAD
        qkv_part = weight_got[:, :, :cut].reshape(groups, nzh, three, 3, PAD)[..., :part]
        qkv_part = qkv_part.transpose(1, 2, 3, 0, 4).reshape(nzh, three, 3 * width)
        out_part = jnp.sum(weight_got[:, :, cut:], axis=0).reshape(nzh, 2, three, width // 2)
        out_part = out_part.transpose(0, 2, 1, 3).reshape(nzh, three, width)
        partial = jnp.concatenate([qkv_part, out_part], axis=2)
        away = lax.dynamic_index_in_dim(partial, 1 - at_zh, 0, keepdims=False).astype(BF16)
        grad_weights = lax.dynamic_index_in_dim(partial, at_zh, 0, keepdims=False)
        grad_weights = grad_weights + lax.ppermute(away, "zh", swap).astype(F32)

    with jax.named_scope("tokens_out"):
        got = exchange(sent[0].reshape(groups, heads * 6 * HEAD, rows), ("x", "c"))
        got = got.reshape(groups, heads, 6, HEAD, rows)
        attended = got[:, :, 0].reshape(width, rows)
        grad_query = got[:, :, 1].reshape(width, rows)
        grad_kv = got[:, :, 2:].reshape(groups, heads, nzh, 2, HEAD, rows).transpose(2, 3, 0, 1, 4, 5)
        grad_kv = grad_kv.reshape(nzh, 2 * width, rows)
        kv_own = lax.dynamic_index_in_dim(grad_kv, at_zh, 0, keepdims=False)
        kv_other = lax.dynamic_index_in_dim(grad_kv, 1 - at_zh, 0, keepdims=False)

        def product(left, right, dims):
            return lax.dot_general(left, right, (dims, ((), ())), preferred_element_type=F32)

        grad_other = product(kv_other, w_qkv[:, width:], ((0,), (1,))).astype(BF16)
        grad_other = lax.ppermute(grad_other, "zh", swap)
        update = product(attended, w_out, ((0,), (0,))).astype(BF16)
        grad_own = product(jnp.concatenate([grad_query, kv_own], axis=0), w_qkv, ((0,), (1,)))
        normed, inverse = layer_norm(act.astype(F32))
        grad_act = norm_backward(grad_own + grad_other.astype(F32), normed, inverse).astype(BF16)

    return (update[None], grad_act[None], grad_pair, grad_weights)


def solution(mesh):
    fine = Mesh(mesh.devices.reshape(4, 2, 4, 4, 2), AXES)
    row, samp = ("x", "zh"), ("y", "zl", "c")
    in_specs = (
        P(samp, row, None),
        P(None, row + samp, None),
        P(),
        P(),
        P(samp, row, None),
    )
    out_specs = (
        P(samp, row, None),
        P(samp, row, None),
        P(None, row + samp, None),
        P(row + samp, None),
    )
    return jax.shard_map(
        per_device, mesh=fine, in_specs=in_specs, out_specs=out_specs, check_vma=False
    )
```

profile of v0, /device:TPU:1, one launch (start us, length us, event | category | flops | bytes accessed | tf_op | source)
XLA Modules:
  0.0 170.6 jit_solution(5142811927315163306)
XLA Ops:
  0.7 7.8 %collective-permute-start = (bf16[128,768]{1,0:T(8,128)(2,1)}, bf16[128,768]{1,0:T(8,128)(2,1)S(1)}, u32[]{:S(2)}, u32[]{:S(2)}) collective-permute-start(bf16[128,768]{1,0:T(8,128)(2,1)} %bitcast.65), channel_id=1, source_target_pairs={{0,32},{32,0},{1,33},{33,1},{2,34},{34,2},{3,35},{35,3},{4,36},{36... | collective-permute-start | bytes 589832 | tf_op jit(solution)/shard_map/rows_in/ppermute | solution.py:384
  8.5 2.0 %broadcast_in_dim.51 = bf16[4,4,2,2,4,1024]{5,4,3,2,1,0:T(4,128)(2,1)} broadcast(bf16[4,2,2,4,1024]{4,3,2,1,0:T(4,128)(2,1)} %bitcast.74), dimensions={0,2,3,4,5} | broadcast | bytes 655360 | tf_op jit(solution)/shard_map/bias_in/broadcast_in_dim | solution.py:394
  10.4 6.8 %all-to-all-start = ((bf16[32,2,4,1024]{3,2,1,0:T(4,128)(2,1)}), bf16[32,2,4,1024]{3,2,1,0:T(4,128)(2,1)S(1)}, u32[]{:S(2)}, u32[]{:S(2)}) async-start(bf16[32,2,4,1024]{3,2,1,0:T(4,128)(2,1)} %bitcast.8), calls=%async_computation | async-start | bytes 1048576 | tf_op jit(solution)/shard_map/bias_in/all_to_all | solution.py:343
  18.3 1.5 collective-permute-start.7
  19.8 3.7 %own_columns.1 = (bf16[768,384]{1,0:T(8,128)(2,1)}, bf16[768,128]{1,0:T(8,128)(2,1)}) custom-call(s32[5]{0:T(128)} %stack.29.place.refs_0_, bf16[768,2304]{1,0:T(8,128)(2,1)} %w_qkv.1, bf16[768,768]{1,0:T(8,128)(2,1)} %w_out.1), custom_call_target="tpu_custom_call" | custom-call | flops 2000000000 | bytes 6000000 | tf_op jit(solution)/shard_map/rows_in/own_columns/pallas_call | solution.py:72
  23.5 2.4 %collective-permute-start.3 = (bf16[3,128,768]{2,1,0:T(8,128)(2,1)S(1)}, bf16[3,128,768]{2,1,0:T(8,128)(2,1)S(1)}, u32[]{:S(2)}, u32[]{:S(2)}) collective-permute-start(bf16[3,128,768]{2,1,0:T(8,128)(2,1)S(1)} %pad_maximum_fusion.refs_0_.refs_4_), channel_id=1, source_target_pairs={{0,128},{64,192},{128,0},{192,64},{1,129},{65,193},{129,1},{193,65... | collective-permute-start | bytes 1769480 | tf_op jit(solution)/shard_map/rows_in/ppermute | solution.py:352
  27.1 3.1 %project.2 = (bf16[2,2,128,768]{3,2,1,0:T(8,128)(2,1)}, bf16[2,576,128]{2,1,0:T(8,128)(2,1)}) custom-call(bf16[3,128,768]{2,1,0:T(8,128)(2,1)} %copy-done.5, bf16[3,128,768]{2,1,0:T(8,128)(2,1)} %collective-permute-done.1.refs_1_.refs_8_, bf16[768,384]{1,0:T(8,128)(2,1)} %get-tuple-element.28.refs_2_.refs_6_, bf16[768,128]{1,0:T(8,128)(2,1)} %get-tuple-element.29.refs_3_.refs_7_), custom_call_target="tpu_custom_call" | custom-call | flops 2000000000 | bytes 6000000 | tf_op jit(solution)/shard_map/project/project/pallas_call | solution.py:118
  30.2 3.8 %all-to-all-done.refs_0_ = bf16[32,2,4,1024]{3,2,1,0:T(4,128)(2,1)S(1)} async-done(((bf16[32,2,4,1024]{3,2,1,0:T(4,128)(2,1)}), bf16[32,2,4,1024]{3,2,1,0:T(4,128)(2,1)S(1)}, u32[]{:S(2)}, u32[]{:S(2)}) %all-to-all-start) | async-done | bytes 524320 | tf_op jit(solution)/shard_map/bias_in/all_to_all | solution.py:343
  36.2 2.8 %collective-permute-start.4 = (bf16[4,32,1024]{2,1,0:T(8,128)(2,1)S(1)}, bf16[4,32,1024]{2,1,0:T(8,128)(2,1)S(1)}, u32[]{:S(2)}, u32[]{:S(2)}) collective-permute-start(bf16[4,32,1024]{2,1,0:T(8,128)(2,1)S(1)} %squeeze.28.refs_2_.refs_5_), channel_id=1, source_target_pairs={{0,24},{8,0},{16,8},{24,16},{1,25},{9,1},{17,9},{25,17},{2,26},{10... | collective-permute-start | bytes 786440 | tf_op jit(solution)/shard_map/bias_in/ppermute | solution.py:352
  39.7 1.3 collective-permute-start.6
  41.9 11.1 %collective-permute-done.2.refs_0_ = bf16[3,128,768]{2,1,0:T(8,128)(2,1)S(1)} collective-permute-done((bf16[3,128,768]{2,1,0:T(8,128)(2,1)S(1)}, bf16[3,128,768]{2,1,0:T(8,128)(2,1)S(1)}, u32[]{:S(2)}, u32[]{:S(2)}) %collective-permute-start.2) | collective-permute-done | bytes 589856 | tf_op jit(solution)/shard_map/rows_in/ppermute | solution.py:352
  56.3 2.8 %collective-permute-start.11 = (bf16[4,32,1024]{2,1,0:T(8,128)(2,1)S(1)}, bf16[4,32,1024]{2,1,0:T(8,128)(2,1)S(1)}, u32[]{:S(2)}, u32[]{:S(2)}) collective-permute-start(bf16[4,32,1024]{2,1,0:T(8,128)(2,1)S(1)} %copy-done.2), channel_id=1, source_target_pairs={{0,24},{8,0},{16,8},{24,16},{1,25},{9,1},{17,9},{25,17},{2,26},{10... | collective-permute-start | bytes 786440 | tf_op jit(solution)/shard_map/bias_in/ppermute | solution.py:352
  61.9 5.7 %project.3 = (bf16[2,2,128,768]{3,2,1,0:T(8,128)(2,1)}, bf16[2,2,128,768]{3,2,1,0:T(8,128)(2,1)}, bf16[2,2,128,768]{3,2,1,0:T(8,128)(2,1)}, bf16[2,576,128]{2,1,...) custom-call(bf16[3,128,768]{2,1,0:T(8,128)(2,1)} %gate.5.refs_0_.refs_5_, ...), custom_call_target="tpu_custom_call" | custom-call | flops 6000000000 | bytes 18000000 | tf_op jit(solution)/shard_map/project/project/pallas_call | solution.py:118
  67.5 8.8 %attention.2 = (bf16[4,2,2,288,128]{4,3,2,1,0:T(8,128)(2,1)}, bf16[4,32,1024]{2,1,0:T(8,128)(2,1)}, bf16[4,32,1024]{2,1,0:T(8,128)(2,1)}, bf16[4,32,1024]{2,1,0:T(8,128)(2,1)}, bf16[4,32,1024]{2,1,0:T(8,128)(2,1)}) custom-call(s32[5]{0:T(128)} %stack.29.place.refs_0_, bf16[2,576,128]{2,1,0:T(8,128)(2,1)} %get-tuple-element.30.refs_1_, ...), custom_call_target="tpu_custom_call" | custom-call | flops 8999999488 | bytes 27000000 | tf_op jit(solution)/shard_map/attention/attention/pallas_call | solution.py:314
  76.3 1.7 collective-permute-start.15
  78.0 1.6 collective-permute-start.16
  81.4 8.8 %attention.3 = (bf16[4,2,2,288,128]{4,3,2,1,0:T(8,128)(2,1)}, bf16[4,32,1024]{2,1,0:T(8,128)(2,1)}, bf16[4,32,1024]{2,1,0:T(8,128)(2,1)}, bf16[4,32,1024]{2,1,0:T(8,128)(2,1)}, bf16[4,32,1024]{2,1,0:T(8,128)(2,1)}) custom-call(s32[5]{0:T(128)} %stack.29.place.refs_0_, ...), custom_call_target="tpu_custom_call", output_to_operand_aliasing={{0}: (9, {})} | custom-call | flops 8999999488 | bytes 27000000 | tf_op jit(solution)/shard_map/attention/attention/pallas_call | solution.py:314
  90.7 1.4 collective-permute-start.19
  92.1 6.9 %all-to-all-start.1 = ((bf16[8,576,128]{2,1,0:T(8,128)(2,1)}), bf16[8,576,128]{2,1,0:T(8,128)(2,1)S(1)}, u32[]{:S(2)}, u32[]{:S(2)}) async-start(bf16[8,576,128]{2,1,0:T(8,128)(2,1)} %bitcast.68), calls=%async_computation.1 | async-start | bytes 2359296 | tf_op jit(solution)/shard_map/tokens_out/all_to_all | solution.py:343
  100.2 5.0 %weight_grads.1 = (bf16[240,384]{1,0:T(8,128)(2,1)}, bf16[240,384]{1,0:T(8,128)(2,1)}, bf16[240,384]{1,0:T(8,128)(2,1)}, bf16[240,384]{1,0:T(8,128)(2,1)}) custom-call(s32[5]{0:T(128)} %stack.29.place.refs_0_, bf16[4,2,2,288,128]{4,3,2,1,0:T(8,128)(2,1)} %get-tuple-element.35.sent, bf16[2,2,128,768]{3,2,1,0:T(8,128)(2,1)} %get-tuple-element.44.refs_0_, ...), custom_call_target="tpu_custom_call" | custom-call | flops 6000000000 | bytes 18000000 | tf_op jit(solution)/shard_map/weights/weight_grads/pallas_call | solution.py:209
  107.2 1.3 collective-permute-start.22
  108.5 2.0 %collective-permute-start.23 = (bf16[240,384]{1,0:T(8,128)(2,1)}, bf16[240,384]{1,0:T(8,128)(2,1)}, u32[]{:S(2)}, u32[]{:S(2)}) collective-permute-start(bf16[240,384]{1,0:T(8,128)(2,1)} %get-tuple-element.51), channel_id=1, source_target_pairs={{0,24},{8,0},{16,8},{24,16},{1,25},{9,1},{17,9},{25,17},{2,26},{10... | collective-permute-start | bytes 552968 | tf_op jit(solution)/shard_map/along_y/ppermute | solution.py:357
  111.7 2.9 %collective-permute-done.21 = bf16[240,384]{1,0:T(8,128)(2,1)S(1)} collective-permute-done((bf16[240,384]{1,0:T(8,128)(2,1)}, bf16[240,384]{1,0:T(8,128)(2,1)S(1)}, u32[]{:S(2)}, u32[]{:S(2)}) %collective-permute-start.21) | collective-permute-done | bytes 184352 | tf_op jit(solution)/shard_map/along_y/ppermute | solution.py:357
  114.6 2.7 %collective-permute-done.22 = bf16[240,384]{1,0:T(8,128)(2,1)} collective-permute-done((bf16[240,384]{1,0:T(8,128)(2,1)}, bf16[240,384]{1,0:T(8,128)(2,1)}, u32[]{:S(2)}, u32[]{:S(2)}) %collective-permute-start.22) | collective-permute-done | bytes 184352 | tf_op jit(solution)/shard_map/along_y/ppermute | solution.py:357
  120.3 1.3 maximum_maximum_fusion
  121.7 8.1 %all-to-all-start.2 = ((bf16[32,8,1600]{2,1,0:T(8,128)(2,1)}), bf16[32,8,1600]{2,1,0:T(8,128)(2,1)S(1)}, u32[]{:S(2)}, u32[]{:S(2)}) async-start(bf16[32,8,1600]{2,1,0:T(8,128)(2,1)} %maximum_maximum_fusion), calls=%async_computation.2 | async-start | bytes 1703936 | tf_op jit(solution)/shard_map/owners/all_to_all | solution.py:343
  129.9 2.7 %fusion.2 = bf16[128,768]{1,0:T(8,128)(2,1)S(1)} fusion(bf16[768,2304]{1,0:T(8,128)(2,1)} %w_qkv.1, bf16[2,1536,128]{2,1,0:T(8,128)(2,1)S(1)} %bitcast.66, s32[]{:T(128)S(6)} %select_n.17), kind=kOutput, calls=%fused_computation.2 | convolution fusion | flops 302088192 | bytes 2949124 | tf_op jit(solution)/shard_map/tokens_out/dot_general | solution.py:464
  132.7 4.5 %collective-permute-start.14 = (bf16[128,768]{1,0:T(8,128)(2,1)S(1)}, bf16[128,768]{1,0:T(8,128)(2,1)S(1)}, u32[]{:S(2)}, u32[]{:S(2)}) collective-permute-start(bf16[128,768]{1,0:T(8,128)(2,1)S(1)} %fusion.2), channel_id=1, source_target_pairs={{0,32},{32,0},{1,33},{33,1},{2,34},{34,2},{3,35},{35,3},{4,36},{36... | collective-permute-start | bytes 589832 | tf_op jit(solution)/shard_map/tokens_out/ppermute | solution.py:467
  138.2 19.0 %collective-permute-done.14 = bf16[128,768]{1,0:T(8,128)(2,1)S(1)} collective-permute-done((bf16[128,768]{1,0:T(8,128)(2,1)S(1)}, bf16[128,768]{1,0:T(8,128)(2,1)S(1)}, u32[]{:S(2)}, u32[]{:S(2)}) %collective-permute-start.14) | collective-permute-done | bytes 196640 | tf_op jit(solution)/shard_map/tokens_out/ppermute | solution.py:467
  157.3 1.4 fusion.22
  159.6 2.3 %all-to-all-done.2 = bf16[32,8,1600]{2,1,0:T(8,128)(2,1)S(1)} async-done(((bf16[32,8,1600]{2,1,0:T(8,128)(2,1)}), bf16[32,8,1600]{2,1,0:T(8,128)(2,1)S(1)}, u32[]{:S(2)}, u32[]{:S(2)}) %all-to-all-start.2) | async-done | bytes 819232 | tf_op jit(solution)/shard_map/owners/all_to_all | solution.py:343
  163.3 4.5 %collective-permute-start.24 = (bf16[3,3072]{1,0:T(4,128)(2,1)S(1)}, bf16[3,3072]{1,0:T(4,128)(2,1)S(1)}, u32[]{:S(2)}, u32[]{:S(2)}) collective-permute-start(bf16[3,3072]{1,0:T(4,128)(2,1)S(1)} %bitcast.77), channel_id=1, source_target_pairs={{0,32},{32,0},{1,33},{33,1},{2,34},{34,2},{3,35},{35,3},{4,36},{36... | collective-permute-start | bytes 55304 | tf_op jit(solution)/shard_map/owners/ppermute | solution.py:451
  (136 shorter events, 27.8 us)
Async XLA Ops:
  0.6 16.6 %copy-start.1 = (bf16[1,128,768]{2,1,0:T(8,128)(2,1)S(1)}, bf16[1,128,768]{2,1,0:T(8,128)(2,1)}, u32[]{:S(2)}) copy-start(bf16[1,128,768]{2,1,0:T(8,128)(2,1)} %param.5) | copy-start | bytes 589828
  0.6 16.6 %copy-start.13 = (bf16[1,128,768]{2,1,0:T(8,128)(2,1)S(1)}, bf16[1,128,768]{2,1,0:T(8,128)(2,1)}, u32[]{:S(2)}) copy-start(bf16[1,128,768]{2,1,0:T(8,128)(2,1)} %param.9) | copy-start | bytes 589828
  0.7 16.6 %collective-permute-start = (bf16[128,768]{1,0:T(8,128)(2,1)}, bf16[128,768]{1,0:T(8,128)(2,1)S(1)}, u32[]{:S(2)}, u32[]{:S(2)}) collective-permute-start(bf16[128,768]{1,0:T(8,128)(2,1)} %bitcast.65), channel_id=1, source_target_pairs={{0,32},{32,0},{1,33},{33,1},{2,34},{34,2},{3,35},{35,3},{4,36},{36... | collective-permute-start | bytes 589832 | tf_op jit(solution)/shard_map/rows_in/ppermute | solution.py:384
  10.4 23.6 %all-to-all-start = ((bf16[32,2,4,1024]{3,2,1,0:T(4,128)(2,1)}), bf16[32,2,4,1024]{3,2,1,0:T(4,128)(2,1)S(1)}, u32[]{:S(2)}, u32[]{:S(2)}) async-start(bf16[32,2,4,1024]{3,2,1,0:T(4,128)(2,1)} %bitcast.8), calls=%async_computation | async-start | bytes 1048576 | tf_op jit(solution)/shard_map/bias_in/all_to_all | solution.py:343
  17.3 9.8 %collective-permute-start.1 = (bf16[3,128,768]{2,1,0:T(8,128)(2,1)S(1)}, bf16[3,128,768]{2,1,0:T(8,128)(2,1)}, u32[]{:S(2)}, u32[]{:S(2)}) collective-permute-start(bf16[3,128,768]{2,1,0:T(8,128)(2,1)S(1)} %pad_maximum_fusion.refs_0_.refs_4_), channel_id=1, source_target_pairs={{0,1},{1,0},{2,3},{3,2},{4,5},{5,4},{6,7},{7,6},{8,9},{9,8},{10,11... | collective-permute-start | bytes 1769480 | tf_op jit(solution)/shard_map/rows_in/ppermute | solution.py:387
  18.3 21.3 %collective-permute-start.7 = (bf16[3,128,768]{2,1,0:T(8,128)(2,1)S(1)}, bf16[3,128,768]{2,1,0:T(8,128)(2,1)S(1)}, u32[]{:S(2)}, u32[]{:S(2)}) collective-permute-start(bf16[3,128,768]{2,1,0:T(8,128)(2,1)S(1)} %pad_maximum_fusion.refs_0_.refs_4_), channel_id=1, source_target_pairs={{0,64},{64,128},{128,192},{192,0},{1,65},{65,129},{129,193},{193,1... | collective-permute-start | bytes 1769480 | tf_op jit(solution)/shard_map/rows_in/ppermute | solution.py:352
  23.5 30.6 %collective-permute-start.3 = (bf16[3,128,768]{2,1,0:T(8,128)(2,1)S(1)}, bf16[3,128,768]{2,1,0:T(8,128)(2,1)S(1)}, u32[]{:S(2)}, u32[]{:S(2)}) collective-permute-start(bf16[3,128,768]{2,1,0:T(8,128)(2,1)S(1)} %pad_maximum_fusion.refs_0_.refs_4_), channel_id=1, source_target_pairs={{0,128},{64,192},{128,0},{192,64},{1,129},{65,193},{129,1},{193,65... | collective-permute-start | bytes 1769480 | tf_op jit(solution)/shard_map/rows_in/ppermute | solution.py:352
  26.0 27.0 %collective-permute-start.2 = (bf16[3,128,768]{2,1,0:T(8,128)(2,1)S(1)}, bf16[3,128,768]{2,1,0:T(8,128)(2,1)S(1)}, u32[]{:S(2)}, u32[]{:S(2)}) collective-permute-start(bf16[3,128,768]{2,1,0:T(8,128)(2,1)S(1)} %pad_maximum_fusion.refs_0_.refs_4_), channel_id=1, source_target_pairs={{0,192},{64,0},{128,64},{192,128},{1,193},{65,1},{129,65},{193,129... | collective-permute-start | bytes 1769480 | tf_op jit(solution)/shard_map/rows_in/ppermute | solution.py:352
  36.2 18.7 %collective-permute-start.4 = (bf16[4,32,1024]{2,1,0:T(8,128)(2,1)S(1)}, bf16[4,32,1024]{2,1,0:T(8,128)(2,1)S(1)}, u32[]{:S(2)}, u32[]{:S(2)}) collective-permute-start(bf16[4,32,1024]{2,1,0:T(8,128)(2,1)S(1)} %squeeze.28.refs_2_.refs_5_), channel_id=1, source_target_pairs={{0,24},{8,0},{16,8},{24,16},{1,25},{9,1},{17,9},{25,17},{2,26},{10... | collective-permute-start | bytes 786440 | tf_op jit(solution)/shard_map/bias_in/ppermute | solution.py:352
  39.1 15.9 %collective-permute-start.5 = (bf16[4,32,1024]{2,1,0:T(8,128)(2,1)S(1)}, bf16[4,32,1024]{2,1,0:T(8,128)(2,1)}, u32[]{:S(2)}, u32[]{:S(2)}) collective-permute-start(bf16[4,32,1024]{2,1,0:T(8,128)(2,1)S(1)} %squeeze.28.refs_2_.refs_5_), channel_id=1, source_target_pairs={{0,16},{8,24},{16,0},{24,8},{1,17},{9,25},{17,1},{25,9},{2,18},{10... | collective-permute-start | bytes 786440 | tf_op jit(solution)/shard_map/bias_in/ppermute | solution.py:352
  39.7 15.3 %collective-permute-start.6 = (bf16[4,32,1024]{2,1,0:T(8,128)(2,1)S(1)}, bf16[4,32,1024]{2,1,0:T(8,128)(2,1)}, u32[]{:S(2)}, u32[]{:S(2)}) collective-permute-start(bf16[4,32,1024]{2,1,0:T(8,128)(2,1)S(1)} %squeeze.28.refs_2_.refs_5_), channel_id=1, source_target_pairs={{0,8},{8,16},{16,24},{24,0},{1,9},{9,17},{17,25},{25,1},{2,10},{10... | collective-permute-start | bytes 786440 | tf_op jit(solution)/shard_map/bias_in/ppermute | solution.py:352
  41.9 14.5 %copy-start.2 = (bf16[4,32,1024]{2,1,0:T(8,128)(2,1)S(1)}, bf16[4,32,1024]{2,1,0:T(8,128)(2,1)}, u32[]{:S(2)}) copy-start(bf16[4,32,1024]{2,1,0:T(8,128)(2,1)} %squeeze.29.refs_3_.refs_5_) | copy-start | bytes 786436
  53.0 6.5 %collective-permute-start.10 = (bf16[3,128,768]{2,1,0:T(8,128)(2,1)}, bf16[3,128,768]{2,1,0:T(8,128)(2,1)S(1)}, u32[]{:S(2)}, u32[]{:S(2)}) collective-permute-start(bf16[3,128,768]{2,1,0:T(8,128)(2,1)} %gate.7.refs_2_.refs_7_), channel_id=1, source_target_pairs={{0,1},{1,0},{2,3},{3,2},{4,5},{5,4},{6,7},{7,6},{8,9},{9,8},{10,11... | collective-permute-start | bytes 1769480 | tf_op jit(solution)/shard_map/project/ppermute | solution.py:403
  54.1 6.1 %collective-permute-start.8 = (bf16[3,128,768]{2,1,0:T(8,128)(2,1)}, bf16[3,128,768]{2,1,0:T(8,128)(2,1)S(1)}, u32[]{:S(2)}, u32[]{:S(2)}) collective-permute-start(bf16[3,128,768]{2,1,0:T(8,128)(2,1)} %gate.5.refs_0_.refs_5_), channel_id=1, source_target_pairs={{0,1},{1,0},{2,3},{3,2},{4,5},{5,4},{6,7},{7,6},{8,9},{9,8},{10,11... | collective-permute-start | bytes 1769480 | tf_op jit(solution)/shard_map/project/ppermute | solution.py:403
  55.7 4.5 %collective-permute-start.9 = (bf16[3,128,768]{2,1,0:T(8,128)(2,1)}, bf16[3,128,768]{2,1,0:T(8,128)(2,1)S(1)}, u32[]{:S(2)}, u32[]{:S(2)}) collective-permute-start(bf16[3,128,768]{2,1,0:T(8,128)(2,1)} %gate.6.refs_1_.refs_6_), channel_id=1, source_target_pairs={{0,1},{1,0},{2,3},{3,2},{4,5},{5,4},{6,7},{7,6},{8,9},{9,8},{10,11... | collective-permute-start | bytes 1769480 | tf_op jit(solution)/shard_map/project/ppermute | solution.py:403
  56.3 23.2 %collective-permute-start.11 = (bf16[4,32,1024]{2,1,0:T(8,128)(2,1)S(1)}, bf16[4,32,1024]{2,1,0:T(8,128)(2,1)S(1)}, u32[]{:S(2)}, u32[]{:S(2)}) collective-permute-start(bf16[4,32,1024]{2,1,0:T(8,128)(2,1)S(1)} %copy-done.2), channel_id=1, source_target_pairs={{0,24},{8,0},{16,8},{24,16},{1,25},{9,1},{17,9},{25,17},{2,26},{10... | collective-permute-start | bytes 786440 | tf_op jit(solution)/shard_map/bias_in/ppermute | solution.py:352
  59.1 21.4 %collective-permute-start.12 = (bf16[4,32,1024]{2,1,0:T(8,128)(2,1)S(1)}, bf16[4,32,1024]{2,1,0:T(8,128)(2,1)S(1)}, u32[]{:S(2)}, u32[]{:S(2)}) collective-permute-start(bf16[4,32,1024]{2,1,0:T(8,128)(2,1)S(1)} %copy-done.2), channel_id=1, source_target_pairs={{0,16},{8,24},{16,0},{24,8},{1,17},{9,25},{17,1},{25,9},{2,18},{10... | collective-permute-start | bytes 786440 | tf_op jit(solution)/shard_map/bias_in/ppermute | solution.py:352
  59.5 21.1 %collective-permute-start.13 = (bf16[4,32,1024]{2,1,0:T(8,128)(2,1)S(1)}, bf16[4,32,1024]{2,1,0:T(8,128)(2,1)S(1)}, u32[]{:S(2)}, u32[]{:S(2)}) collective-permute-start(bf16[4,32,1024]{2,1,0:T(8,128)(2,1)S(1)} %copy-done.2), channel_id=1, source_target_pairs={{0,8},{8,16},{16,24},{24,0},{1,9},{9,17},{17,25},{25,1},{2,10},{10... | collective-permute-start | bytes 786440 | tf_op jit(solution)/shard_map/bias_in/ppermute | solution.py:352
  76.3 22.7 %collective-permute-start.15 = (bf16[4,32,1024]{2,1,0:T(8,128)(2,1)}, bf16[4,32,1024]{2,1,0:T(8,128)(2,1)S(1)}, u32[]{:S(2)}, u32[]{:S(2)}) collective-permute-start(bf16[4,32,1024]{2,1,0:T(8,128)(2,1)} %get-tuple-element.37), channel_id=1, source_target_pairs={{0,8},{8,16},{16,24},{24,0},{1,9},{9,17},{17,25},{25,1},{2,10},{10... | collective-permute-start | bytes 786440 | tf_op jit(solution)/shard_map/along_y/ppermute | solution.py:357
  78.0 27.2 %collective-permute-start.16 = (bf16[4,32,1024]{2,1,0:T(8,128)(2,1)}, bf16[4,32,1024]{2,1,0:T(8,128)(2,1)S(1)}, u32[]{:S(2)}, u32[]{:S(2)}) collective-permute-start(bf16[4,32,1024]{2,1,0:T(8,128)(2,1)} %get-tuple-element.38), channel_id=1, source_target_pairs={{0,16},{8,24},{16,0},{24,8},{1,17},{9,25},{17,1},{25,9},{2,18},{10... | collective-permute-start | bytes 786440 | tf_op jit(solution)/shard_map/along_y/ppermute | solution.py:357
  79.5 25.6 %collective-permute-start.17 = (bf16[4,32,1024]{2,1,0:T(8,128)(2,1)}, bf16[4,32,1024]{2,1,0:T(8,128)(2,1)S(1)}, u32[]{:S(2)}, u32[]{:S(2)}) collective-permute-start(bf16[4,32,1024]{2,1,0:T(8,128)(2,1)} %get-tuple-element.39), channel_id=1, source_target_pairs={{0,24},{8,0},{16,8},{24,16},{1,25},{9,1},{17,9},{25,17},{2,26},{10... | collective-permute-start | bytes 786440 | tf_op jit(solution)/shard_map/along_y/ppermute | solution.py:357
  90.2 18.4 %collective-permute-start.18 = (bf16[4,32,1024]{2,1,0:T(8,128)(2,1)}, bf16[4,32,1024]{2,1,0:T(8,128)(2,1)S(1)}, u32[]{:S(2)}, u32[]{:S(2)}) collective-permute-start(bf16[4,32,1024]{2,1,0:T(8,128)(2,1)} %get-tuple-element.41), channel_id=1, source_target_pairs={{0,8},{8,16},{16,24},{24,0},{1,9},{9,17},{17,25},{25,1},{2,10},{10... | collective-permute-start | bytes 786440 | tf_op jit(solution)/shard_map/along_y/ppermute | solution.py:357
  90.7 19.8 %collective-permute-start.19 = (bf16[4,32,1024]{2,1,0:T(8,128)(2,1)}, bf16[4,32,1024]{2,1,0:T(8,128)(2,1)S(1)}, u32[]{:S(2)}, u32[]{:S(2)}) collective-permute-start(bf16[4,32,1024]{2,1,0:T(8,128)(2,1)} %get-tuple-element.42), channel_id=1, source_target_pairs={{0,16},{8,24},{16,0},{24,8},{1,17},{9,25},{17,1},{25,9},{2,18},{10... | collective-permute-start | bytes 786440 | tf_op jit(solution)/shard_map/along_y/ppermute | solution.py:357
  92.1 29.6 %all-to-all-start.1 = ((bf16[8,576,128]{2,1,0:T(8,128)(2,1)}), bf16[8,576,128]{2,1,0:T(8,128)(2,1)S(1)}, u32[]{:S(2)}, u32[]{:S(2)}) async-start(bf16[8,576,128]{2,1,0:T(8,128)(2,1)} %bitcast.68), calls=%async_computation.1 | async-start | bytes 2359296 | tf_op jit(solution)/shard_map/tokens_out/all_to_all | solution.py:343
  99.0 11.5 %collective-permute-start.20 = (bf16[4,32,1024]{2,1,0:T(8,128)(2,1)}, bf16[4,32,1024]{2,1,0:T(8,128)(2,1)}, u32[]{:S(2)}, u32[]{:S(2)}) collective-permute-start(bf16[4,32,1024]{2,1,0:T(8,128)(2,1)} %get-tuple-element.43), channel_id=1, source_target_pairs={{0,24},{8,0},{16,8},{24,16},{1,25},{9,1},{17,9},{25,17},{2,26},{10... | collective-permute-start | bytes 786440 | tf_op jit(solution)/shard_map/along_y/ppermute | solution.py:357
  106.5 8.1 %collective-permute-start.21 = (bf16[240,384]{1,0:T(8,128)(2,1)}, bf16[240,384]{1,0:T(8,128)(2,1)S(1)}, u32[]{:S(2)}, u32[]{:S(2)}) collective-permute-start(bf16[240,384]{1,0:T(8,128)(2,1)} %get-tuple-element.49), channel_id=1, source_target_pairs={{0,8},{8,16},{16,24},{24,0},{1,9},{9,17},{17,25},{25,1},{2,10},{10... | collective-permute-start | bytes 552968 | tf_op jit(solution)/shard_map/along_y/ppermute | solution.py:357
  107.2 10.1 %collective-permute-start.22 = (bf16[240,384]{1,0:T(8,128)(2,1)}, bf16[240,384]{1,0:T(8,128)(2,1)}, u32[]{:S(2)}, u32[]{:S(2)}) collective-permute-start(bf16[240,384]{1,0:T(8,128)(2,1)} %get-tuple-element.50), channel_id=1, source_target_pairs={{0,16},{8,24},{16,0},{24,8},{1,17},{9,25},{17,1},{25,9},{2,18},{10... | collective-permute-start | bytes 552968 | tf_op jit(solution)/shard_map/along_y/ppermute | solution.py:357
  108.5 9.7 %collective-permute-start.23 = (bf16[240,384]{1,0:T(8,128)(2,1)}, bf16[240,384]{1,0:T(8,128)(2,1)}, u32[]{:S(2)}, u32[]{:S(2)}) collective-permute-start(bf16[240,384]{1,0:T(8,128)(2,1)} %get-tuple-element.51), channel_id=1, source_target_pairs={{0,24},{8,0},{16,8},{24,16},{1,25},{9,1},{17,9},{25,17},{2,26},{10... | collective-permute-start | bytes 552968 | tf_op jit(solution)/shard_map/along_y/ppermute | solution.py:357
  121.7 40.2 %all-to-all-start.2 = ((bf16[32,8,1600]{2,1,0:T(8,128)(2,1)}), bf16[32,8,1600]{2,1,0:T(8,128)(2,1)S(1)}, u32[]{:S(2)}, u32[]{:S(2)}) async-start(bf16[32,8,1600]{2,1,0:T(8,128)(2,1)} %maximum_maximum_fusion), calls=%async_computation.2 | async-start | bytes 1703936 | tf_op jit(solution)/shard_map/owners/all_to_all | solution.py:343
  129.9 27.4 %copy-start.15 = (bf16[768,2304]{1,0:T(8,128)(2,1)S(1)}, bf16[768,2304]{1,0:T(8,128)(2,1)}, u32[]{:S(2)}) copy-start(bf16[768,2304]{1,0:T(8,128)(2,1)} %w_qkv.1) | copy-start | bytes 10616836
  132.7 24.6 %collective-permute-start.14 = (bf16[128,768]{1,0:T(8,128)(2,1)S(1)}, bf16[128,768]{1,0:T(8,128)(2,1)S(1)}, u32[]{:S(2)}, u32[]{:S(2)}) collective-permute-start(bf16[128,768]{1,0:T(8,128)(2,1)S(1)} %fusion.2), channel_id=1, source_target_pairs={{0,32},{32,0},{1,33},{33,1},{2,34},{34,2},{3,35},{35,3},{4,36},{36... | collective-permute-start | bytes 589832 | tf_op jit(solution)/shard_map/tokens_out/ppermute | solution.py:467
  163.3 6.7 %collective-permute-start.24 = (bf16[3,3072]{1,0:T(4,128)(2,1)S(1)}, bf16[3,3072]{1,0:T(4,128)(2,1)S(1)}, u32[]{:S(2)}, u32[]{:S(2)}) collective-permute-start(bf16[3,3072]{1,0:T(4,128)(2,1)S(1)} %bitcast.77), channel_id=1, source_target_pairs={{0,32},{32,0},{1,33},{33,1},{2,34},{34,2},{3,35},{35,3},{4,36},{36... | collective-permute-start | bytes 55304 | tf_op jit(solution)/shard_map/owners/ppermute | solution.py:451
  (18 other events, 55.7 us)
where the time goes:
time: 171 us
  starting transfers between devices  65.8 us (38%)
  waiting for transfers between devices  44 us (26%)
  Pallas kernels  35 us (20%)
  local copies, waits for them, and re-layouts  11.3 us (7%)
  other arithmetic  8.1 us (5%)
  matrix products  5.21 us (3%)
    all_to_all x3, starting transfers between devices, exchange(): return lax.all_to_all(values, axes, split_axis=0, concat_axis=0, tiled=True)  21.7 us
    ppermute x1, waiting for transfers between devices, per_device(): grad_other = lax.ppermute(grad_other, 'zh', swap)  19 us
    pallas_call x2, Pallas kernels, attention(): pl.pallas_call(lambda *refs: attention_kernel(scale, *refs), grid=(nx //...  17.5 us
    ppermute x9, starting transfers between devices, around(): lax.ppermute(values, axis, ring(n, -shift))  13.4 us
    ppermute x9, waiting for transfers between devices, around(): lax.ppermute(values, axis, ring(n, -shift))  11.4 us
    ppermute x9, starting transfers between devices, ring_scatter(): lax.ppermute(pieces[shift], axis, ring(n, shift))  11.3 us
    pallas_call x2, Pallas kernels, project(): pl.pallas_call(lambda *refs: project_kernel(number, *refs), in_specs=[who...  8.8 us
    ppermute x1, starting transfers between devices, per_device(): act_other = lax.ppermute(act, 'zh', swap)  7.83 us
  transfers between devices with their start and end apart: 28, of which 9 were waited for; matrix products, arithmetic and copies ran while one was open for 11% of the time, Pallas kernels for 21%

commit v1 on v0

--- a/solution.py
+++ b/solution.py
@@ -397,9 +397,7 @@
         bias = [around(got[:, :, h].reshape(nx, chunk, total), "y") for h in range(heads)]
 
     with jax.named_scope("project"):
-        ready = [first[1], bias[0][0], bias[1][0]]
-        ready = [[], ready, bias[0][1:], ready]
-        pieces = pieces[:1] + [gate(pieces[i], *ready[i]) for i in range(1, nx)]
+        pieces = [pieces[0], pieces[1], gate(pieces[2], *bias[0][1:]), pieces[3]]
         twins = [twin] + [lax.ppermute(piece, "c", swap) for piece in pieces[1:]]
         later = project(pieces[1:], twins[1:], columns, rows_out)
         normed = first[:1] + later[: nx - 1]

time: 171 us -> 169 us (0.988)
  starting transfers between devices: 65.8 us -> 61.9 us
  waiting for transfers between devices: 44 us -> 46.3 us
    ppermute x9, waiting for transfers between devices: 11.4 us -> 13.1 us  [around(): lax.ppermute(values, axis, ring(n, -shift))]
where the time goes in v1:
time: 169 us; the launch traced here: 168 us
  starting transfers between devices  61.9 us (37%)
  waiting for transfers between devices  46.3 us (27%)
  Pallas kernels  35.1 us (21%)
  local copies, waits for them, and re-layouts  10.6 us (6%)
  other arithmetic  8.1 us (5%)
  matrix products  5.21 us (3%)
    all_to_all x3, starting transfers between devices, exchange(): return lax.all_to_all(values, axes, split_axis=0, concat_axis=0, tiled=True)  21.4 us
    ppermute x1, waiting for transfers between devices, per_device(): grad_other = lax.ppermute(grad_other, 'zh', swap)  19 us
    pallas_call x2, Pallas kernels, attention(): pl.pallas_call(lambda *refs: attention_kernel(scale, *refs), grid=(nx //...  17.6 us
    ppermute x9, waiting for transfers between devices, around(): lax.ppermute(values, axis, ring(n, -shift))  13.1 us
    ppermute x9, starting transfers between devices, around(): lax.ppermute(values, axis, ring(n, -shift))  13.1 us
    ppermute x9, starting transfers between devices, ring_scatter(): lax.ppermute(pieces[shift], axis, ring(n, shift))  11.6 us
    pallas_call x2, Pallas kernels, project(): pl.pallas_call(lambda *refs: project_kernel(number, *refs), in_specs=[who...  8.8 us
    ppermute x1, starting transfers between devices, per_device(): act_other = lax.ppermute(act, 'zh', swap)  7.83 us
  transfers between devices with their start and end apart: 28, of which 9 were waited for; matrix products, arithmetic and copies ran while one was open for 11% of the time, Pallas kernels for 21%

profile of v1, /device:TPU:1, one launch (start us, length us, event | category | flops | bytes accessed | tf_op | source)
XLA Modules:
  0.0 168.3 jit_solution(15575216129301359193)
XLA Ops:
  0.7 7.8 %collective-permute-start = (bf16[128,768]{1,0:T(8,128)(2,1)}, bf16[128,768]{1,0:T(8,128)(2,1)S(1)}, u32[]{:S(2)}, u32[]{:S(2)}) collective-permute-start(bf16[128,768]{1,0:T(8,128)(2,1)} %bitcast.65), channel_id=1, source_target_pairs={{0,32},{32,0},{1,33},{33,1},{2,34},{34,2},{3,35},{35,3},{4,36},{36... | collective-permute-start | bytes 589832 | tf_op jit(solution)/shard_map/rows_in/ppermute | solution.py:384
  8.5 2.0 %broadcast_in_dim.51 = bf16[4,4,2,2,4,1024]{5,4,3,2,1,0:T(4,128)(2,1)} broadcast(bf16[4,2,2,4,1024]{4,3,2,1,0:T(4,128)(2,1)} %bitcast.74), dimensions={0,2,3,4,5} | broadcast | bytes 655360 | tf_op jit(solution)/shard_map/bias_in/broadcast_in_dim | solution.py:394
  10.4 6.8 %all-to-all-start = ((bf16[32,2,4,1024]{3,2,1,0:T(4,128)(2,1)}), bf16[32,2,4,1024]{3,2,1,0:T(4,128)(2,1)S(1)}, u32[]{:S(2)}, u32[]{:S(2)}) async-start(bf16[32,2,4,1024]{3,2,1,0:T(4,128)(2,1)} %bitcast.8), calls=%async_computation | async-start | bytes 1048576 | tf_op jit(solution)/shard_map/bias_in/all_to_all | solution.py:343
  18.3 3.0 %collective-permute-start.3 = (bf16[3,128,768]{2,1,0:T(8,128)(2,1)S(1)}, bf16[3,128,768]{2,1,0:T(8,128)(2,1)S(1)}, u32[]{:S(2)}, u32[]{:S(2)}) collective-permute-start(bf16[3,128,768]{2,1,0:T(8,128)(2,1)S(1)} %pad_maximum_fusion.refs_0_.refs_4_), channel_id=1, source_target_pairs={{0,128},{64,192},{128,0},{192,64},{1,129},{65,193},{129,1},{193,65... | collective-permute-start | bytes 1769480 | tf_op jit(solution)/shard_map/rows_in/ppermute | solution.py:352
  21.3 3.7 %own_columns.1 = (bf16[768,384]{1,0:T(8,128)(2,1)}, bf16[768,128]{1,0:T(8,128)(2,1)}) custom-call(s32[5]{0:T(128)} %stack.29.place.refs_0_, bf16[768,2304]{1,0:T(8,128)(2,1)} %w_qkv.1, bf16[768,768]{1,0:T(8,128)(2,1)} %w_out.1), custom_call_target="tpu_custom_call" | custom-call | flops 2000000000 | bytes 6000000 | tf_op jit(solution)/shard_map/rows_in/own_columns/pallas_call | solution.py:72
  25.4 2.4 %collective-permute-start.2 = (bf16[3,128,768]{2,1,0:T(8,128)(2,1)S(1)}, bf16[3,128,768]{2,1,0:T(8,128)(2,1)}, u32[]{:S(2)}, u32[]{:S(2)}) collective-permute-start(bf16[3,128,768]{2,1,0:T(8,128)(2,1)S(1)} %pad_maximum_fusion.refs_0_.refs_4_), channel_id=1, source_target_pairs={{0,192},{64,0},{128,64},{192,128},{1,193},{65,1},{129,65},{193,129... | collective-permute-start | bytes 1769480 | tf_op jit(solution)/shard_map/rows_in/ppermute | solution.py:352
  28.5 3.1 %project.2 = (bf16[2,2,128,768]{3,2,1,0:T(8,128)(2,1)}, bf16[2,576,128]{2,1,0:T(8,128)(2,1)}) custom-call(bf16[3,128,768]{2,1,0:T(8,128)(2,1)} %copy-done.3, bf16[3,128,768]{2,1,0:T(8,128)(2,1)} %copy-done.16, bf16[768,384]{1,0:T(8,128)(2,1)} %get-tuple-element.28.refs_2_.refs_6_, bf16[768,128]{1,0:T(8,128)(2,1)} %get-tuple-element.29.refs_3_.refs_7_), custom_call_target="tpu_custom_call" | custom-call | flops 2000000000 | bytes 6000000 | tf_op jit(solution)/shard_map/project/project/pallas_call | solution.py:118
  31.7 2.4 %all-to-all-done.refs_0_ = bf16[32,2,4,1024]{3,2,1,0:T(4,128)(2,1)S(1)} async-done(((bf16[32,2,4,1024]{3,2,1,0:T(4,128)(2,1)}), bf16[32,2,4,1024]{3,2,1,0:T(4,128)(2,1)S(1)}, u32[]{:S(2)}, u32[]{:S(2)}) %all-to-all-start) | async-done | bytes 524320 | tf_op jit(solution)/shard_map/bias_in/all_to_all | solution.py:343
  36.3 2.8 %collective-permute-start.4 = (bf16[4,32,1024]{2,1,0:T(8,128)(2,1)S(1)}, bf16[4,32,1024]{2,1,0:T(8,128)(2,1)S(1)}, u32[]{:S(2)}, u32[]{:S(2)}) collective-permute-start(bf16[4,32,1024]{2,1,0:T(8,128)(2,1)S(1)} %squeeze.28.refs_5_), channel_id=1, source_target_pairs={{0,24},{8,0},{16,8},{24,16},{1,25},{9,1},{17,9},{25,17},{2,26},{10... | collective-permute-start | bytes 786440 | tf_op jit(solution)/shard_map/bias_in/ppermute | solution.py:352
  40.8 11.5 %collective-permute-done.7.refs_2_.refs_7_ = bf16[3,128,768]{2,1,0:T(8,128)(2,1)S(1)} collective-permute-done((bf16[3,128,768]{2,1,0:T(8,128)(2,1)S(1)}, bf16[3,128,768]{2,1,0:T(8,128)(2,1)S(1)}, u32[]{:S(2)}, u32[]{:S(2)}) %collective-permute-start.7) | collective-permute-done | bytes 589856 | tf_op jit(solution)/shard_map/rows_in/ppermute | solution.py:352
  52.9 1.6 collective-permute-done.6.refs_3_.refs_8_
  56.2 2.0 %collective-permute-start.11 = (bf16[4,32,1024]{2,1,0:T(8,128)(2,1)S(1)}, bf16[4,32,1024]{2,1,0:T(8,128)(2,1)S(1)}, u32[]{:S(2)}, u32[]{:S(2)}) collective-permute-start(bf16[4,32,1024]{2,1,0:T(8,128)(2,1)S(1)} %squeeze.29.refs_5_), channel_id=1, source_target_pairs={{0,24},{8,0},{16,8},{24,16},{1,25},{9,1},{17,9},{25,17},{2,26},{10... | collective-permute-start | bytes 786440 | tf_op jit(solution)/shard_map/bias_in/ppermute | solution.py:352
  60.0 5.7 %project.3 = (bf16[2,2,128,768]{3,2,1,0:T(8,128)(2,1)}, bf16[2,2,128,768]{3,2,1,0:T(8,128)(2,1)}, bf16[2,2,128,768]{3,2,1,0:T(8,128)(2,1)}, bf16[2,576,128]{2,1,...) custom-call(bf16[3,128,768]{2,1,0:T(8,128)(2,1)} %collective-permute-done.2.refs_0_.refs_5_, ...), custom_call_target="tpu_custom_call" | custom-call | flops 6000000000 | bytes 18000000 | tf_op jit(solution)/shard_map/project/project/pallas_call | solution.py:118
  65.7 8.8 %attention.2 = (bf16[4,2,2,288,128]{4,3,2,1,0:T(8,128)(2,1)}, bf16[4,32,1024]{2,1,0:T(8,128)(2,1)}, bf16[4,32,1024]{2,1,0:T(8,128)(2,1)}, bf16[4,32,1024]{2,1,0:T(8,128)(2,1)}, bf16[4,32,1024]{2,1,0:T(8,128)(2,1)}) custom-call(s32[5]{0:T(128)} %stack.29.place.refs_0_, bf16[2,576,128]{2,1,0:T(8,128)(2,1)} %get-tuple-element.30.refs_1_, ...), custom_call_target="tpu_custom_call" | custom-call | flops 8999999488 | bytes 27000000 | tf_op jit(solution)/shard_map/attention/attention/pallas_call | solution.py:314
  74.5 1.7 %collective-permute-start.15 = (bf16[4,32,1024]{2,1,0:T(8,128)(2,1)}, bf16[4,32,1024]{2,1,0:T(8,128)(2,1)S(1)}, u32[]{:S(2)}, u32[]{:S(2)}) collective-permute-start(bf16[4,32,1024]{2,1,0:T(8,128)(2,1)} %get-tuple-element.37), channel_id=1, source_target_pairs={{0,8},{8,16},{16,24},{24,0},{1,9},{9,17},{17,25},{25,1},{2,10},{10... | collective-permute-start | bytes 786440 | tf_op jit(solution)/shard_map/along_y/ppermute | solution.py:357
  76.2 1.6 collective-permute-start.16
  79.6 8.8 %attention.3 = (bf16[4,2,2,288,128]{4,3,2,1,0:T(8,128)(2,1)}, bf16[4,32,1024]{2,1,0:T(8,128)(2,1)}, bf16[4,32,1024]{2,1,0:T(8,128)(2,1)}, bf16[4,32,1024]{2,1,0:T(8,128)(2,1)}, bf16[4,32,1024]{2,1,0:T(8,128)(2,1)}) custom-call(s32[5]{0:T(128)} %stack.29.place.refs_0_, ...), custom_call_target="tpu_custom_call", output_to_operand_aliasing={{0}: (9, {})} | custom-call | flops 8999999488 | bytes 27000000 | tf_op jit(solution)/shard_map/attention/attention/pallas_call | solution.py:314
  88.9 1.4 collective-permute-start.19
  90.3 5.8 %all-to-all-start.1 = ((bf16[8,576,128]{2,1,0:T(8,128)(2,1)}), bf16[8,576,128]{2,1,0:T(8,128)(2,1)S(1)}, u32[]{:S(2)}, u32[]{:S(2)}) async-start(bf16[8,576,128]{2,1,0:T(8,128)(2,1)} %bitcast.68), calls=%async_computation.1 | async-start | bytes 2359296 | tf_op jit(solution)/shard_map/tokens_out/all_to_all | solution.py:343
  97.2 5.0 %weight_grads.1 = (bf16[240,384]{1,0:T(8,128)(2,1)}, bf16[240,384]{1,0:T(8,128)(2,1)}, bf16[240,384]{1,0:T(8,128)(2,1)}, bf16[240,384]{1,0:T(8,128)(2,1)}) custom-call(s32[5]{0:T(128)} %stack.29.place.refs_0_, bf16[4,2,2,288,128]{4,3,2,1,0:T(8,128)(2,1)} %get-tuple-element.35.sent, bf16[2,2,128,768]{3,2,1,0:T(8,128)(2,1)} %get-tuple-element.44.refs_0_, ...), custom_call_target="tpu_custom_call" | custom-call | flops 6000000000 | bytes 18000000 | tf_op jit(solution)/shard_map/weights/weight_grads/pallas_call | solution.py:209
  105.8 2.0 %collective-permute-start.23 = (bf16[240,384]{1,0:T(8,128)(2,1)}, bf16[240,384]{1,0:T(8,128)(2,1)}, u32[]{:S(2)}, u32[]{:S(2)}) collective-permute-start(bf16[240,384]{1,0:T(8,128)(2,1)} %get-tuple-element.51), channel_id=1, source_target_pairs={{0,24},{8,0},{16,8},{24,16},{1,25},{9,1},{17,9},{25,17},{2,26},{10... | collective-permute-start | bytes 552968 | tf_op jit(solution)/shard_map/along_y/ppermute | solution.py:357
  109.0 2.3 %collective-permute-done.21 = bf16[240,384]{1,0:T(8,128)(2,1)S(1)} collective-permute-done((bf16[240,384]{1,0:T(8,128)(2,1)}, bf16[240,384]{1,0:T(8,128)(2,1)S(1)}, u32[]{:S(2)}, u32[]{:S(2)}) %collective-permute-start.21) | collective-permute-done | bytes 184352 | tf_op jit(solution)/shard_map/along_y/ppermute | solution.py:357
  111.3 3.2 %collective-permute-done.22 = bf16[240,384]{1,0:T(8,128)(2,1)} collective-permute-done((bf16[240,384]{1,0:T(8,128)(2,1)}, bf16[240,384]{1,0:T(8,128)(2,1)}, u32[]{:S(2)}, u32[]{:S(2)}) %collective-permute-start.22) | collective-permute-done | bytes 184352 | tf_op jit(solution)/shard_map/along_y/ppermute | solution.py:357
  117.3 1.3 maximum_maximum_fusion
  118.6 8.9 %all-to-all-start.2 = ((bf16[32,8,1600]{2,1,0:T(8,128)(2,1)}), bf16[32,8,1600]{2,1,0:T(8,128)(2,1)S(1)}, u32[]{:S(2)}, u32[]{:S(2)}) async-start(bf16[32,8,1600]{2,1,0:T(8,128)(2,1)} %maximum_maximum_fusion), calls=%async_computation.2 | async-start | bytes 1703936 | tf_op jit(solution)/shard_map/owners/all_to_all | solution.py:343
  127.7 2.8 %fusion.2 = bf16[128,768]{1,0:T(8,128)(2,1)S(1)} fusion(bf16[768,2304]{1,0:T(8,128)(2,1)} %w_qkv.1, bf16[2,1536,128]{2,1,0:T(8,128)(2,1)S(1)} %bitcast.66, s32[]{:T(128)S(6)} %select_n.17), kind=kOutput, calls=%fused_computation.2 | convolution fusion | flops 302088192 | bytes 2949124 | tf_op jit(solution)/shard_map/tokens_out/dot_general | solution.py:462
  130.4 3.3 %collective-permute-start.14 = (bf16[128,768]{1,0:T(8,128)(2,1)S(1)}, bf16[128,768]{1,0:T(8,128)(2,1)S(1)}, u32[]{:S(2)}, u32[]{:S(2)}) collective-permute-start(bf16[128,768]{1,0:T(8,128)(2,1)S(1)} %fusion.2), channel_id=1, source_target_pairs={{0,32},{32,0},{1,33},{33,1},{2,34},{34,2},{3,35},{35,3},{4,36},{36... | collective-permute-start | bytes 589832 | tf_op jit(solution)/shard_map/tokens_out/ppermute | solution.py:465
  134.9 19.0 %collective-permute-done.14 = bf16[128,768]{1,0:T(8,128)(2,1)S(1)} collective-permute-done((bf16[128,768]{1,0:T(8,128)(2,1)S(1)}, bf16[128,768]{1,0:T(8,128)(2,1)S(1)}, u32[]{:S(2)}, u32[]{:S(2)}) %collective-permute-start.14) | collective-permute-done | bytes 196640 | tf_op jit(solution)/shard_map/tokens_out/ppermute | solution.py:465
  153.9 1.4 fusion.22
  156.2 3.4 %all-to-all-done.2 = bf16[32,8,1600]{2,1,0:T(8,128)(2,1)S(1)} async-done(((bf16[32,8,1600]{2,1,0:T(8,128)(2,1)}), bf16[32,8,1600]{2,1,0:T(8,128)(2,1)S(1)}, u32[]{:S(2)}, u32[]{:S(2)}) %all-to-all-start.2) | async-done | bytes 819232 | tf_op jit(solution)/shard_map/owners/all_to_all | solution.py:343
  161.0 3.3 %collective-permute-start.24 = (bf16[3,3072]{1,0:T(4,128)(2,1)S(1)}, bf16[3,3072]{1,0:T(4,128)(2,1)S(1)}, u32[]{:S(2)}, u32[]{:S(2)}) collective-permute-start(bf16[3,3072]{1,0:T(4,128)(2,1)S(1)} %bitcast.77), channel_id=1, source_target_pairs={{0,32},{32,0},{1,33},{33,1},{2,34},{34,2},{3,35},{35,3},{4,36},{36... | collective-permute-start | bytes 55304 | tf_op jit(solution)/shard_map/owners/ppermute | solution.py:449
  165.6 2.1 %collective-permute-done.24 = bf16[3,3072]{1,0:T(4,128)(2,1)S(1)} collective-permute-done((bf16[3,3072]{1,0:T(4,128)(2,1)S(1)}, bf16[3,3072]{1,0:T(4,128)(2,1)S(1)}, u32[]{:S(2)}, u32[]{:S(2)}) %collective-permute-start.24) | collective-permute-done | bytes 18464 | tf_op jit(solution)/shard_map/owners/ppermute | solution.py:449
  (134 shorter events, 26.5 us)
Async XLA Ops:
  0.6 16.6 %copy-start.1 = (bf16[1,128,768]{2,1,0:T(8,128)(2,1)S(1)}, bf16[1,128,768]{2,1,0:T(8,128)(2,1)}, u32[]{:S(2)}) copy-start(bf16[1,128,768]{2,1,0:T(8,128)(2,1)} %param.5) | copy-start | bytes 589828
  0.6 16.6 %copy-start.13 = (bf16[1,128,768]{2,1,0:T(8,128)(2,1)S(1)}, bf16[1,128,768]{2,1,0:T(8,128)(2,1)}, u32[]{:S(2)}) copy-start(bf16[1,128,768]{2,1,0:T(8,128)(2,1)} %param.9) | copy-start | bytes 589828
  0.7 16.6 %collective-permute-start = (bf16[128,768]{1,0:T(8,128)(2,1)}, bf16[128,768]{1,0:T(8,128)(2,1)S(1)}, u32[]{:S(2)}, u32[]{:S(2)}) collective-permute-start(bf16[128,768]{1,0:T(8,128)(2,1)} %bitcast.65), channel_id=1, source_target_pairs={{0,32},{32,0},{1,33},{33,1},{2,34},{34,2},{3,35},{35,3},{4,36},{36... | collective-permute-start | bytes 589832 | tf_op jit(solution)/shard_map/rows_in/ppermute | solution.py:384
  10.4 23.7 %all-to-all-start = ((bf16[32,2,4,1024]{3,2,1,0:T(4,128)(2,1)}), bf16[32,2,4,1024]{3,2,1,0:T(4,128)(2,1)S(1)}, u32[]{:S(2)}, u32[]{:S(2)}) async-start(bf16[32,2,4,1024]{3,2,1,0:T(4,128)(2,1)} %bitcast.8), calls=%async_computation | async-start | bytes 1048576 | tf_op jit(solution)/shard_map/bias_in/all_to_all | solution.py:343
  17.3 10.4 %collective-permute-start.1 = (bf16[3,128,768]{2,1,0:T(8,128)(2,1)S(1)}, bf16[3,128,768]{2,1,0:T(8,128)(2,1)S(1)}, u32[]{:S(2)}, u32[]{:S(2)}) collective-permute-start(bf16[3,128,768]{2,1,0:T(8,128)(2,1)S(1)} %pad_maximum_fusion.refs_0_.refs_4_), channel_id=1, source_target_pairs={{0,1},{1,0},{2,3},{3,2},{4,5},{5,4},{6,7},{7,6},{8,9},{9,8},{10,11... | collective-permute-start | bytes 1769480 | tf_op jit(solution)/shard_map/rows_in/ppermute | solution.py:387
  18.3 21.1 %collective-permute-start.3 = (bf16[3,128,768]{2,1,0:T(8,128)(2,1)S(1)}, bf16[3,128,768]{2,1,0:T(8,128)(2,1)S(1)}, u32[]{:S(2)}, u32[]{:S(2)}) collective-permute-start(bf16[3,128,768]{2,1,0:T(8,128)(2,1)S(1)} %pad_maximum_fusion.refs_0_.refs_4_), channel_id=1, source_target_pairs={{0,128},{64,192},{128,0},{192,64},{1,129},{65,193},{129,1},{193,65... | collective-permute-start | bytes 1769480 | tf_op jit(solution)/shard_map/rows_in/ppermute | solution.py:352
  25.0 27.3 %collective-permute-start.7 = (bf16[3,128,768]{2,1,0:T(8,128)(2,1)S(1)}, bf16[3,128,768]{2,1,0:T(8,128)(2,1)S(1)}, u32[]{:S(2)}, u32[]{:S(2)}) collective-permute-start(bf16[3,128,768]{2,1,0:T(8,128)(2,1)S(1)} %pad_maximum_fusion.refs_0_.refs_4_), channel_id=1, source_target_pairs={{0,64},{64,128},{128,192},{192,0},{1,65},{65,129},{129,193},{193,1... | collective-permute-start | bytes 1769480 | tf_op jit(solution)/shard_map/rows_in/ppermute | solution.py:352
  25.4 27.4 %collective-permute-start.2 = (bf16[3,128,768]{2,1,0:T(8,128)(2,1)S(1)}, bf16[3,128,768]{2,1,0:T(8,128)(2,1)}, u32[]{:S(2)}, u32[]{:S(2)}) collective-permute-start(bf16[3,128,768]{2,1,0:T(8,128)(2,1)S(1)} %pad_maximum_fusion.refs_0_.refs_4_), channel_id=1, source_target_pairs={{0,192},{64,0},{128,64},{192,128},{1,193},{65,1},{129,65},{193,129... | collective-permute-start | bytes 1769480 | tf_op jit(solution)/shard_map/rows_in/ppermute | solution.py:352
  36.3 29.4 %copy-start.11 = (bf16[4,32,1024]{2,1,0:T(8,128)(2,1)}, bf16[4,32,1024]{2,1,0:T(8,128)(2,1)S(1)}, u32[]{:S(2)}) copy-start(bf16[4,32,1024]{2,1,0:T(8,128)(2,1)S(1)} %squeeze.28.refs_5_) | copy-start | bytes 786436
  36.3 16.6 %collective-permute-start.4 = (bf16[4,32,1024]{2,1,0:T(8,128)(2,1)S(1)}, bf16[4,32,1024]{2,1,0:T(8,128)(2,1)S(1)}, u32[]{:S(2)}, u32[]{:S(2)}) collective-permute-start(bf16[4,32,1024]{2,1,0:T(8,128)(2,1)S(1)} %squeeze.28.refs_5_), channel_id=1, source_target_pairs={{0,24},{8,0},{16,8},{24,16},{1,25},{9,1},{17,9},{25,17},{2,26},{10... | collective-permute-start | bytes 786440 | tf_op jit(solution)/shard_map/bias_in/ppermute | solution.py:352
  39.1 13.8 %collective-permute-start.5 = (bf16[4,32,1024]{2,1,0:T(8,128)(2,1)S(1)}, bf16[4,32,1024]{2,1,0:T(8,128)(2,1)S(1)}, u32[]{:S(2)}, u32[]{:S(2)}) collective-permute-start(bf16[4,32,1024]{2,1,0:T(8,128)(2,1)S(1)} %squeeze.28.refs_5_), channel_id=1, source_target_pairs={{0,16},{8,24},{16,0},{24,8},{1,17},{9,25},{17,1},{25,9},{2,18},{10... | collective-permute-start | bytes 786440 | tf_op jit(solution)/shard_map/bias_in/ppermute | solution.py:352
  39.5 15.0 %collective-permute-start.6 = (bf16[4,32,1024]{2,1,0:T(8,128)(2,1)S(1)}, bf16[4,32,1024]{2,1,0:T(8,128)(2,1)S(1)}, u32[]{:S(2)}, u32[]{:S(2)}) collective-permute-start(bf16[4,32,1024]{2,1,0:T(8,128)(2,1)S(1)} %squeeze.28.refs_5_), channel_id=1, source_target_pairs={{0,8},{8,16},{16,24},{24,0},{1,9},{9,17},{17,25},{25,1},{2,10},{10... | collective-permute-start | bytes 786440 | tf_op jit(solution)/shard_map/bias_in/ppermute | solution.py:352
  52.3 6.1 %collective-permute-start.10 = (bf16[3,128,768]{2,1,0:T(8,128)(2,1)S(1)}, bf16[3,128,768]{2,1,0:T(8,128)(2,1)}, u32[]{:S(2)}, u32[]{:S(2)}) collective-permute-start(bf16[3,128,768]{2,1,0:T(8,128)(2,1)S(1)} %collective-permute-done.7.refs_2_.refs_7_), channel_id=1, source_target_pairs={{0,1},{1,0},{2,3},{3,2},{4,5},{5,4},{6,7},{7,6},{8,9},{9,8},{10,11... | collective-permute-start | bytes 1769480 | tf_op jit(solution)/shard_map/project/ppermute | solution.py:401
  52.8 6.4 %collective-permute-start.8 = (bf16[3,128,768]{2,1,0:T(8,128)(2,1)}, bf16[3,128,768]{2,1,0:T(8,128)(2,1)}, u32[]{:S(2)}, u32[]{:S(2)}) collective-permute-start(bf16[3,128,768]{2,1,0:T(8,128)(2,1)} %collective-permute-done.2.refs_0_.refs_5_), channel_id=1, source_target_pairs={{0,1},{1,0},{2,3},{3,2},{4,5},{5,4},{6,7},{7,6},{8,9},{9,8},{10,11... | collective-permute-start | bytes 1769480 | tf_op jit(solution)/shard_map/project/ppermute | solution.py:401
  55.2 4.0 %collective-permute-start.9 = (bf16[3,128,768]{2,1,0:T(8,128)(2,1)}, bf16[3,128,768]{2,1,0:T(8,128)(2,1)S(1)}, u32[]{:S(2)}, u32[]{:S(2)}) collective-permute-start(bf16[3,128,768]{2,1,0:T(8,128)(2,1)} %gate.3.refs_1_.refs_6_), channel_id=1, source_target_pairs={{0,1},{1,0},{2,3},{3,2},{4,5},{5,4},{6,7},{7,6},{8,9},{9,8},{10,11... | collective-permute-start | bytes 1769480 | tf_op jit(solution)/shard_map/project/ppermute | solution.py:401
  56.2 21.6 %collective-permute-start.11 = (bf16[4,32,1024]{2,1,0:T(8,128)(2,1)S(1)}, bf16[4,32,1024]{2,1,0:T(8,128)(2,1)S(1)}, u32[]{:S(2)}, u32[]{:S(2)}) collective-permute-start(bf16[4,32,1024]{2,1,0:T(8,128)(2,1)S(1)} %squeeze.29.refs_5_), channel_id=1, source_target_pairs={{0,24},{8,0},{16,8},{24,16},{1,25},{9,1},{17,9},{25,17},{2,26},{10... | collective-permute-start | bytes 786440 | tf_op jit(solution)/shard_map/bias_in/ppermute | solution.py:352
  58.1 20.7 %collective-permute-start.12 = (bf16[4,32,1024]{2,1,0:T(8,128)(2,1)S(1)}, bf16[4,32,1024]{2,1,0:T(8,128)(2,1)S(1)}, u32[]{:S(2)}, u32[]{:S(2)}) collective-permute-start(bf16[4,32,1024]{2,1,0:T(8,128)(2,1)S(1)} %squeeze.29.refs_5_), channel_id=1, source_target_pairs={{0,16},{8,24},{16,0},{24,8},{1,17},{9,25},{17,1},{25,9},{2,18},{10... | collective-permute-start | bytes 786440 | tf_op jit(solution)/shard_map/bias_in/ppermute | solution.py:352
  58.5 20.3 %collective-permute-start.13 = (bf16[4,32,1024]{2,1,0:T(8,128)(2,1)S(1)}, bf16[4,32,1024]{2,1,0:T(8,128)(2,1)S(1)}, u32[]{:S(2)}, u32[]{:S(2)}) collective-permute-start(bf16[4,32,1024]{2,1,0:T(8,128)(2,1)S(1)} %squeeze.29.refs_5_), channel_id=1, source_target_pairs={{0,8},{8,16},{16,24},{24,0},{1,9},{9,17},{17,25},{25,1},{2,10},{10... | collective-permute-start | bytes 786440 | tf_op jit(solution)/shard_map/bias_in/ppermute | solution.py:352
  74.5 21.6 %collective-permute-start.15 = (bf16[4,32,1024]{2,1,0:T(8,128)(2,1)}, bf16[4,32,1024]{2,1,0:T(8,128)(2,1)S(1)}, u32[]{:S(2)}, u32[]{:S(2)}) collective-permute-start(bf16[4,32,1024]{2,1,0:T(8,128)(2,1)} %get-tuple-element.37), channel_id=1, source_target_pairs={{0,8},{8,16},{16,24},{24,0},{1,9},{9,17},{17,25},{25,1},{2,10},{10... | collective-permute-start | bytes 786440 | tf_op jit(solution)/shard_map/along_y/ppermute | solution.py:357
  76.2 26.1 %collective-permute-start.16 = (bf16[4,32,1024]{2,1,0:T(8,128)(2,1)}, bf16[4,32,1024]{2,1,0:T(8,128)(2,1)S(1)}, u32[]{:S(2)}, u32[]{:S(2)}) collective-permute-start(bf16[4,32,1024]{2,1,0:T(8,128)(2,1)} %get-tuple-element.38), channel_id=1, source_target_pairs={{0,16},{8,24},{16,0},{24,8},{1,17},{9,25},{17,1},{25,9},{2,18},{10... | collective-permute-start | bytes 786440 | tf_op jit(solution)/shard_map/along_y/ppermute | solution.py:357
  77.7 24.5 %collective-permute-start.17 = (bf16[4,32,1024]{2,1,0:T(8,128)(2,1)}, bf16[4,32,1024]{2,1,0:T(8,128)(2,1)S(1)}, u32[]{:S(2)}, u32[]{:S(2)}) collective-permute-start(bf16[4,32,1024]{2,1,0:T(8,128)(2,1)} %get-tuple-element.39), channel_id=1, source_target_pairs={{0,24},{8,0},{16,8},{24,16},{1,25},{9,1},{17,9},{25,17},{2,26},{10... | collective-permute-start | bytes 786440 | tf_op jit(solution)/shard_map/along_y/ppermute | solution.py:357
  88.4 17.4 %collective-permute-start.18 = (bf16[4,32,1024]{2,1,0:T(8,128)(2,1)}, bf16[4,32,1024]{2,1,0:T(8,128)(2,1)S(1)}, u32[]{:S(2)}, u32[]{:S(2)}) collective-permute-start(bf16[4,32,1024]{2,1,0:T(8,128)(2,1)} %get-tuple-element.41), channel_id=1, source_target_pairs={{0,8},{8,16},{16,24},{24,0},{1,9},{9,17},{17,25},{25,1},{2,10},{10... | collective-permute-start | bytes 786440 | tf_op jit(solution)/shard_map/along_y/ppermute | solution.py:357
  88.9 18.9 %collective-permute-start.19 = (bf16[4,32,1024]{2,1,0:T(8,128)(2,1)}, bf16[4,32,1024]{2,1,0:T(8,128)(2,1)S(1)}, u32[]{:S(2)}, u32[]{:S(2)}) collective-permute-start(bf16[4,32,1024]{2,1,0:T(8,128)(2,1)} %get-tuple-element.42), channel_id=1, source_target_pairs={{0,16},{8,24},{16,0},{24,8},{1,17},{9,25},{17,1},{25,9},{2,18},{10... | collective-permute-start | bytes 786440 | tf_op jit(solution)/shard_map/along_y/ppermute | solution.py:357
  90.3 28.3 %all-to-all-start.1 = ((bf16[8,576,128]{2,1,0:T(8,128)(2,1)}), bf16[8,576,128]{2,1,0:T(8,128)(2,1)S(1)}, u32[]{:S(2)}, u32[]{:S(2)}) async-start(bf16[8,576,128]{2,1,0:T(8,128)(2,1)} %bitcast.68), calls=%async_computation.1 | async-start | bytes 2359296 | tf_op jit(solution)/shard_map/tokens_out/all_to_all | solution.py:343
  96.1 11.7 %collective-permute-start.20 = (bf16[4,32,1024]{2,1,0:T(8,128)(2,1)}, bf16[4,32,1024]{2,1,0:T(8,128)(2,1)}, u32[]{:S(2)}, u32[]{:S(2)}) collective-permute-start(bf16[4,32,1024]{2,1,0:T(8,128)(2,1)} %get-tuple-element.43), channel_id=1, source_target_pairs={{0,24},{8,0},{16,8},{24,16},{1,25},{9,1},{17,9},{25,17},{2,26},{10... | collective-permute-start | bytes 786440 | tf_op jit(solution)/shard_map/along_y/ppermute | solution.py:357
  103.5 7.7 %collective-permute-start.21 = (bf16[240,384]{1,0:T(8,128)(2,1)}, bf16[240,384]{1,0:T(8,128)(2,1)S(1)}, u32[]{:S(2)}, u32[]{:S(2)}) collective-permute-start(bf16[240,384]{1,0:T(8,128)(2,1)} %get-tuple-element.49), channel_id=1, source_target_pairs={{0,8},{8,16},{16,24},{24,0},{1,9},{9,17},{17,25},{25,1},{2,10},{10... | collective-permute-start | bytes 552968 | tf_op jit(solution)/shard_map/along_y/ppermute | solution.py:357
  104.5 9.9 %collective-permute-start.22 = (bf16[240,384]{1,0:T(8,128)(2,1)}, bf16[240,384]{1,0:T(8,128)(2,1)}, u32[]{:S(2)}, u32[]{:S(2)}) collective-permute-start(bf16[240,384]{1,0:T(8,128)(2,1)} %get-tuple-element.50), channel_id=1, source_target_pairs={{0,16},{8,24},{16,0},{24,8},{1,17},{9,25},{17,1},{25,9},{2,18},{10... | collective-permute-start | bytes 552968 | tf_op jit(solution)/shard_map/along_y/ppermute | solution.py:357
  105.8 9.4 %collective-permute-start.23 = (bf16[240,384]{1,0:T(8,128)(2,1)}, bf16[240,384]{1,0:T(8,128)(2,1)}, u32[]{:S(2)}, u32[]{:S(2)}) collective-permute-start(bf16[240,384]{1,0:T(8,128)(2,1)} %get-tuple-element.51), channel_id=1, source_target_pairs={{0,24},{8,0},{16,8},{24,16},{1,25},{9,1},{17,9},{25,17},{2,26},{10... | collective-permute-start | bytes 552968 | tf_op jit(solution)/shard_map/along_y/ppermute | solution.py:357
  118.6 41.0 %all-to-all-start.2 = ((bf16[32,8,1600]{2,1,0:T(8,128)(2,1)}), bf16[32,8,1600]{2,1,0:T(8,128)(2,1)S(1)}, u32[]{:S(2)}, u32[]{:S(2)}) async-start(bf16[32,8,1600]{2,1,0:T(8,128)(2,1)} %maximum_maximum_fusion), calls=%async_computation.2 | async-start | bytes 1703936 | tf_op jit(solution)/shard_map/owners/all_to_all | solution.py:343
  127.6 26.2 %copy-start.15 = (bf16[768,2304]{1,0:T(8,128)(2,1)S(1)}, bf16[768,2304]{1,0:T(8,128)(2,1)}, u32[]{:S(2)}) copy-start(bf16[768,2304]{1,0:T(8,128)(2,1)} %w_qkv.1) | copy-start | bytes 10616836
  130.4 23.5 %collective-permute-start.14 = (bf16[128,768]{1,0:T(8,128)(2,1)S(1)}, bf16[128,768]{1,0:T(8,128)(2,1)S(1)}, u32[]{:S(2)}, u32[]{:S(2)}) collective-permute-start(bf16[128,768]{1,0:T(8,128)(2,1)S(1)} %fusion.2), channel_id=1, source_target_pairs={{0,32},{32,0},{1,33},{33,1},{2,34},{34,2},{3,35},{35,3},{4,36},{36... | collective-permute-start | bytes 589832 | tf_op jit(solution)/shard_map/tokens_out/ppermute | solution.py:465
  161.0 6.7 %collective-permute-start.24 = (bf16[3,3072]{1,0:T(4,128)(2,1)S(1)}, bf16[3,3072]{1,0:T(4,128)(2,1)S(1)}, u32[]{:S(2)}, u32[]{:S(2)}) collective-permute-start(bf16[3,3072]{1,0:T(4,128)(2,1)S(1)} %bitcast.77), channel_id=1, source_target_pairs={{0,32},{32,0},{1,33},{33,1},{2,34},{34,2},{3,35},{35,3},{4,36},{36... | collective-permute-start | bytes 55304 | tf_op jit(solution)/shard_map/owners/ppermute | solution.py:449
  (18 other events, 78.0 us)

commit v2 on v1

--- a/solution.py
+++ b/solution.py
@@ -283,8 +283,8 @@
         else:
             pair[...] += grad_score
         dq = (jnp.dot(score_b, k_all[t], preferred_element_type=F32) * scale).T
-        dk_acc[t] += jnp.dot(q_t, score_b, preferred_element_type=F32)
-        dv_acc[t] += jnp.dot(g_t, probs_b, preferred_element_type=F32)
+        dk_acc[t] += jnp.dot(q_t[:HEAD], score_b, preferred_element_type=F32)
+        dv_acc[t] += jnp.dot(g_t[:HEAD], probs_b, preferred_element_type=F32)
         for x in range(wide):
             send_ref[step * wide + x, s, 0, :HEAD] = att[:HEAD, x * rows : (x + 1) * rows].astype(BF16)
             send_ref[step * wide + x, s, 0, HEAD : 2 * HEAD] = dq[:HEAD, x * rows : (x + 1) * rows].astype(BF16)
@@ -330,8 +330,8 @@
             pltpu.VMEM((2, total, PAD), BF16),
             pltpu.VMEM((2, PAD, nx * rows), BF16),
             pltpu.VMEM((2, PAD, nx * rows), BF16),
-            pltpu.VMEM((2, PAD, total), F32),
-            pltpu.VMEM((2, PAD, total), F32),
+            pltpu.VMEM((2, HEAD, total), F32),
+            pltpu.VMEM((2, HEAD, total), F32),
         ],
         compiler_params=pltpu.CompilerParams(vmem_limit_bytes=VMEM_LIMIT),
         cost_estimate=cost(9),

time: 169 us -> 169 us (level)
  no operation moved by 1% of the time
where the time goes in v2:
time: 169 us; the launch traced here: 168 us
  starting transfers between devices  62 us (37%)
  waiting for transfers between devices  46.4 us (27%)
  Pallas kernels  34.9 us (21%)
  local copies, waits for them, and re-layouts  10.6 us (6%)
  other arithmetic  8.1 us (5%)
  matrix products  5.21 us (3%)
    all_to_all x3, starting transfers between devices, exchange(): return lax.all_to_all(values, axes, split_axis=0, concat_axis=0, tiled=True)  21.4 us
    ppermute x1, waiting for transfers between devices, per_device(): grad_other = lax.ppermute(grad_other, 'zh', swap)  19 us
    pallas_call x2, Pallas kernels, attention(): pl.pallas_call(lambda *refs: attention_kernel(scale, *refs), grid=(nx //...  17.4 us
    ppermute x9, waiting for transfers between devices, around(): lax.ppermute(values, axis, ring(n, -shift))  13.1 us
    ppermute x9, starting transfers between devices, around(): lax.ppermute(values, axis, ring(n, -shift))  13.1 us
    ppermute x9, starting transfers between devices, ring_scatter(): lax.ppermute(pieces[shift], axis, ring(n, shift))  11.8 us
    pallas_call x2, Pallas kernels, project(): pl.pallas_call(lambda *refs: project_kernel(number, *refs), in_specs=[who...  8.8 us
    ppermute x1, starting transfers between devices, per_device(): act_other = lax.ppermute(act, 'zh', swap)  7.83 us
  transfers between devices with their start and end apart: 28, of which 9 were waited for; matrix products, arithmetic and copies ran while one was open for 11% of the time, Pallas kernels for 21%

profile of v2, /device:TPU:1, one launch (start us, length us, event | category | flops | bytes accessed | tf_op | source)
XLA Modules:
  0.0 168.4 jit_solution(9461420348452210677)
XLA Ops:
  0.7 7.8 %collective-permute-start = (bf16[128,768]{1,0:T(8,128)(2,1)}, bf16[128,768]{1,0:T(8,128)(2,1)S(1)}, u32[]{:S(2)}, u32[]{:S(2)}) collective-permute-start(bf16[128,768]{1,0:T(8,128)(2,1)} %bitcast.65), channel_id=1, source_target_pairs={{0,32},{32,0},{1,33},{33,1},{2,34},{34,2},{3,35},{35,3},{4,36},{36... | collective-permute-start | bytes 589832 | tf_op jit(solution)/shard_map/rows_in/ppermute | solution.py:384
  8.5 2.0 %broadcast_in_dim.51 = bf16[4,4,2,2,4,1024]{5,4,3,2,1,0:T(4,128)(2,1)} broadcast(bf16[4,2,2,4,1024]{4,3,2,1,0:T(4,128)(2,1)} %bitcast.74), dimensions={0,2,3,4,5} | broadcast | bytes 655360 | tf_op jit(solution)/shard_map/bias_in/broadcast_in_dim | solution.py:394
  10.4 6.8 %all-to-all-start = ((bf16[32,2,4,1024]{3,2,1,0:T(4,128)(2,1)}), bf16[32,2,4,1024]{3,2,1,0:T(4,128)(2,1)S(1)}, u32[]{:S(2)}, u32[]{:S(2)}) async-start(bf16[32,2,4,1024]{3,2,1,0:T(4,128)(2,1)} %bitcast.8), calls=%async_computation | async-start | bytes 1048576 | tf_op jit(solution)/shard_map/bias_in/all_to_all | solution.py:343
  18.3 3.0 %collective-permute-start.3 = (bf16[3,128,768]{2,1,0:T(8,128)(2,1)S(1)}, bf16[3,128,768]{2,1,0:T(8,128)(2,1)S(1)}, u32[]{:S(2)}, u32[]{:S(2)}) collective-permute-start(bf16[3,128,768]{2,1,0:T(8,128)(2,1)S(1)} %pad_maximum_fusion.refs_0_.refs_4_), channel_id=1, source_target_pairs={{0,128},{64,192},{128,0},{192,64},{1,129},{65,193},{129,1},{193,65... | collective-permute-start | bytes 1769480 | tf_op jit(solution)/shard_map/rows_in/ppermute | solution.py:352
  21.3 3.7 %own_columns.1 = (bf16[768,384]{1,0:T(8,128)(2,1)}, bf16[768,128]{1,0:T(8,128)(2,1)}) custom-call(s32[5]{0:T(128)} %stack.29.place.refs_0_, bf16[768,2304]{1,0:T(8,128)(2,1)} %w_qkv.1, bf16[768,768]{1,0:T(8,128)(2,1)} %w_out.1), custom_call_target="tpu_custom_call" | custom-call | flops 2000000000 | bytes 6000000 | tf_op jit(solution)/shard_map/rows_in/own_columns/pallas_call | solution.py:72
  25.4 2.4 %collective-permute-start.2 = (bf16[3,128,768]{2,1,0:T(8,128)(2,1)S(1)}, bf16[3,128,768]{2,1,0:T(8,128)(2,1)}, u32[]{:S(2)}, u32[]{:S(2)}) collective-permute-start(bf16[3,128,768]{2,1,0:T(8,128)(2,1)S(1)} %pad_maximum_fusion.refs_0_.refs_4_), channel_id=1, source_target_pairs={{0,192},{64,0},{128,64},{192,128},{1,193},{65,1},{129,65},{193,129... | collective-permute-start | bytes 1769480 | tf_op jit(solution)/shard_map/rows_in/ppermute | solution.py:352
  28.5 3.1 %project.2 = (bf16[2,2,128,768]{3,2,1,0:T(8,128)(2,1)}, bf16[2,576,128]{2,1,0:T(8,128)(2,1)}) custom-call(bf16[3,128,768]{2,1,0:T(8,128)(2,1)} %copy-done.3, bf16[3,128,768]{2,1,0:T(8,128)(2,1)} %copy-done.16, bf16[768,384]{1,0:T(8,128)(2,1)} %get-tuple-element.28.refs_2_.refs_6_, bf16[768,128]{1,0:T(8,128)(2,1)} %get-tuple-element.29.refs_3_.refs_7_), custom_call_target="tpu_custom_call" | custom-call | flops 2000000000 | bytes 6000000 | tf_op jit(solution)/shard_map/project/project/pallas_call | solution.py:118
  31.7 2.4 %all-to-all-done.refs_0_ = bf16[32,2,4,1024]{3,2,1,0:T(4,128)(2,1)S(1)} async-done(((bf16[32,2,4,1024]{3,2,1,0:T(4,128)(2,1)}), bf16[32,2,4,1024]{3,2,1,0:T(4,128)(2,1)S(1)}, u32[]{:S(2)}, u32[]{:S(2)}) %all-to-all-start) | async-done | bytes 524320 | tf_op jit(solution)/shard_map/bias_in/all_to_all | solution.py:343
  36.3 2.8 %collective-permute-start.4 = (bf16[4,32,1024]{2,1,0:T(8,128)(2,1)S(1)}, bf16[4,32,1024]{2,1,0:T(8,128)(2,1)S(1)}, u32[]{:S(2)}, u32[]{:S(2)}) collective-permute-start(bf16[4,32,1024]{2,1,0:T(8,128)(2,1)S(1)} %squeeze.28.refs_5_), channel_id=1, source_target_pairs={{0,24},{8,0},{16,8},{24,16},{1,25},{9,1},{17,9},{25,17},{2,26},{10... | collective-permute-start | bytes 786440 | tf_op jit(solution)/shard_map/bias_in/ppermute | solution.py:352
  40.8 11.5 %collective-permute-done.7.refs_2_.refs_7_ = bf16[3,128,768]{2,1,0:T(8,128)(2,1)S(1)} collective-permute-done((bf16[3,128,768]{2,1,0:T(8,128)(2,1)S(1)}, bf16[3,128,768]{2,1,0:T(8,128)(2,1)S(1)}, u32[]{:S(2)}, u32[]{:S(2)}) %collective-permute-start.7) | collective-permute-done | bytes 589856 | tf_op jit(solution)/shard_map/rows_in/ppermute | solution.py:352
  52.9 1.6 collective-permute-done.6.refs_3_.refs_8_
  56.2 2.0 %collective-permute-start.11 = (bf16[4,32,1024]{2,1,0:T(8,128)(2,1)S(1)}, bf16[4,32,1024]{2,1,0:T(8,128)(2,1)S(1)}, u32[]{:S(2)}, u32[]{:S(2)}) collective-permute-start(bf16[4,32,1024]{2,1,0:T(8,128)(2,1)S(1)} %squeeze.29.refs_5_), channel_id=1, source_target_pairs={{0,24},{8,0},{16,8},{24,16},{1,25},{9,1},{17,9},{25,17},{2,26},{10... | collective-permute-start | bytes 786440 | tf_op jit(solution)/shard_map/bias_in/ppermute | solution.py:352
  60.0 5.7 %project.3 = (bf16[2,2,128,768]{3,2,1,0:T(8,128)(2,1)}, bf16[2,2,128,768]{3,2,1,0:T(8,128)(2,1)}, bf16[2,2,128,768]{3,2,1,0:T(8,128)(2,1)}, bf16[2,576,128]{2,1,...) custom-call(bf16[3,128,768]{2,1,0:T(8,128)(2,1)} %collective-permute-done.2.refs_0_.refs_5_, ...), custom_call_target="tpu_custom_call" | custom-call | flops 6000000000 | bytes 18000000 | tf_op jit(solution)/shard_map/project/project/pallas_call | solution.py:118
  65.7 8.7 %attention.2 = (bf16[4,2,2,288,128]{4,3,2,1,0:T(8,128)(2,1)}, bf16[4,32,1024]{2,1,0:T(8,128)(2,1)}, bf16[4,32,1024]{2,1,0:T(8,128)(2,1)}, bf16[4,32,1024]{2,1,0:T(8,128)(2,1)}, bf16[4,32,1024]{2,1,0:T(8,128)(2,1)}) custom-call(s32[5]{0:T(128)} %stack.29.place.refs_0_, bf16[2,576,128]{2,1,0:T(8,128)(2,1)} %get-tuple-element.30.refs_1_, ...), custom_call_target="tpu_custom_call" | custom-call | flops 8999999488 | bytes 27000000 | tf_op jit(solution)/shard_map/attention/attention/pallas_call | solution.py:314
  74.4 1.7 %collective-permute-start.15 = (bf16[4,32,1024]{2,1,0:T(8,128)(2,1)}, bf16[4,32,1024]{2,1,0:T(8,128)(2,1)S(1)}, u32[]{:S(2)}, u32[]{:S(2)}) collective-permute-start(bf16[4,32,1024]{2,1,0:T(8,128)(2,1)} %get-tuple-element.37), channel_id=1, source_target_pairs={{0,8},{8,16},{16,24},{24,0},{1,9},{9,17},{17,25},{25,1},{2,10},{10... | collective-permute-start | bytes 786440 | tf_op jit(solution)/shard_map/along_y/ppermute | solution.py:357
  76.1 1.6 collective-permute-start.16
  79.5 8.7 %attention.3 = (bf16[4,2,2,288,128]{4,3,2,1,0:T(8,128)(2,1)}, bf16[4,32,1024]{2,1,0:T(8,128)(2,1)}, bf16[4,32,1024]{2,1,0:T(8,128)(2,1)}, bf16[4,32,1024]{2,1,0:T(8,128)(2,1)}, bf16[4,32,1024]{2,1,0:T(8,128)(2,1)}) custom-call(s32[5]{0:T(128)} %stack.29.place.refs_0_, ...), custom_call_target="tpu_custom_call", output_to_operand_aliasing={{0}: (9, {})} | custom-call | flops 8999999488 | bytes 27000000 | tf_op jit(solution)/shard_map/attention/attention/pallas_call | solution.py:314
  88.7 1.4 collective-permute-start.19
  90.1 5.8 %all-to-all-start.1 = ((bf16[8,576,128]{2,1,0:T(8,128)(2,1)}), bf16[8,576,128]{2,1,0:T(8,128)(2,1)S(1)}, u32[]{:S(2)}, u32[]{:S(2)}) async-start(bf16[8,576,128]{2,1,0:T(8,128)(2,1)} %bitcast.68), calls=%async_computation.1 | async-start | bytes 2359296 | tf_op jit(solution)/shard_map/tokens_out/all_to_all | solution.py:343
  97.3 5.0 %weight_grads.1 = (bf16[240,384]{1,0:T(8,128)(2,1)}, bf16[240,384]{1,0:T(8,128)(2,1)}, bf16[240,384]{1,0:T(8,128)(2,1)}, bf16[240,384]{1,0:T(8,128)(2,1)}) custom-call(s32[5]{0:T(128)} %stack.29.place.refs_0_, bf16[4,2,2,288,128]{4,3,2,1,0:T(8,128)(2,1)} %get-tuple-element.35.sent, bf16[2,2,128,768]{3,2,1,0:T(8,128)(2,1)} %get-tuple-element.44.refs_0_, ...), custom_call_target="tpu_custom_call" | custom-call | flops 6000000000 | bytes 18000000 | tf_op jit(solution)/shard_map/weights/weight_grads/pallas_call | solution.py:209
  104.4 1.5 collective-permute-start.22
  105.9 2.0 %collective-permute-start.23 = (bf16[240,384]{1,0:T(8,128)(2,1)}, bf16[240,384]{1,0:T(8,128)(2,1)}, u32[]{:S(2)}, u32[]{:S(2)}) collective-permute-start(bf16[240,384]{1,0:T(8,128)(2,1)} %get-tuple-element.51), channel_id=1, source_target_pairs={{0,24},{8,0},{16,8},{24,16},{1,25},{9,1},{17,9},{25,17},{2,26},{10... | collective-permute-start | bytes 552968 | tf_op jit(solution)/shard_map/along_y/ppermute | solution.py:357
  109.1 2.3 %collective-permute-done.21 = bf16[240,384]{1,0:T(8,128)(2,1)S(1)} collective-permute-done((bf16[240,384]{1,0:T(8,128)(2,1)}, bf16[240,384]{1,0:T(8,128)(2,1)S(1)}, u32[]{:S(2)}, u32[]{:S(2)}) %collective-permute-start.21) | collective-permute-done | bytes 184352 | tf_op jit(solution)/shard_map/along_y/ppermute | solution.py:357
  111.4 3.1 %collective-permute-done.22 = bf16[240,384]{1,0:T(8,128)(2,1)} collective-permute-done((bf16[240,384]{1,0:T(8,128)(2,1)}, bf16[240,384]{1,0:T(8,128)(2,1)}, u32[]{:S(2)}, u32[]{:S(2)}) %collective-permute-start.22) | collective-permute-done | bytes 184352 | tf_op jit(solution)/shard_map/along_y/ppermute | solution.py:357
  118.7 8.9 %all-to-all-start.2 = ((bf16[32,8,1600]{2,1,0:T(8,128)(2,1)}), bf16[32,8,1600]{2,1,0:T(8,128)(2,1)S(1)}, u32[]{:S(2)}, u32[]{:S(2)}) async-start(bf16[32,8,1600]{2,1,0:T(8,128)(2,1)} %maximum_maximum_fusion), calls=%async_computation.2 | async-start | bytes 1703936 | tf_op jit(solution)/shard_map/owners/all_to_all | solution.py:343
  127.7 2.8 %fusion.2 = bf16[128,768]{1,0:T(8,128)(2,1)S(1)} fusion(bf16[768,2304]{1,0:T(8,128)(2,1)} %w_qkv.1, bf16[2,1536,128]{2,1,0:T(8,128)(2,1)S(1)} %bitcast.66, s32[]{:T(128)S(6)} %select_n.17), kind=kOutput, calls=%fused_computation.2 | convolution fusion | flops 302088192 | bytes 2949124 | tf_op jit(solution)/shard_map/tokens_out/dot_general | solution.py:462
  130.5 3.3 %collective-permute-start.14 = (bf16[128,768]{1,0:T(8,128)(2,1)S(1)}, bf16[128,768]{1,0:T(8,128)(2,1)S(1)}, u32[]{:S(2)}, u32[]{:S(2)}) collective-permute-start(bf16[128,768]{1,0:T(8,128)(2,1)S(1)} %fusion.2), channel_id=1, source_target_pairs={{0,32},{32,0},{1,33},{33,1},{2,34},{34,2},{3,35},{35,3},{4,36},{36... | collective-permute-start | bytes 589832 | tf_op jit(solution)/shard_map/tokens_out/ppermute | solution.py:465
  134.9 19.0 %collective-permute-done.14 = bf16[128,768]{1,0:T(8,128)(2,1)S(1)} collective-permute-done((bf16[128,768]{1,0:T(8,128)(2,1)S(1)}, bf16[128,768]{1,0:T(8,128)(2,1)S(1)}, u32[]{:S(2)}, u32[]{:S(2)}) %collective-permute-start.14) | collective-permute-done | bytes 196640 | tf_op jit(solution)/shard_map/tokens_out/ppermute | solution.py:465
  153.9 1.4 fusion.22
  156.2 3.5 %all-to-all-done.2 = bf16[32,8,1600]{2,1,0:T(8,128)(2,1)S(1)} async-done(((bf16[32,8,1600]{2,1,0:T(8,128)(2,1)}), bf16[32,8,1600]{2,1,0:T(8,128)(2,1)S(1)}, u32[]{:S(2)}, u32[]{:S(2)}) %all-to-all-start.2) | async-done | bytes 819232 | tf_op jit(solution)/shard_map/owners/all_to_all | solution.py:343
  161.1 3.3 %collective-permute-start.24 = (bf16[3,3072]{1,0:T(4,128)(2,1)S(1)}, bf16[3,3072]{1,0:T(4,128)(2,1)S(1)}, u32[]{:S(2)}, u32[]{:S(2)}) collective-permute-start(bf16[3,3072]{1,0:T(4,128)(2,1)S(1)} %bitcast.77), channel_id=1, source_target_pairs={{0,32},{32,0},{1,33},{33,1},{2,34},{34,2},{3,35},{35,3},{4,36},{36... | collective-permute-start | bytes 55304 | tf_op jit(solution)/shard_map/owners/ppermute | solution.py:449
  165.7 2.1 %collective-permute-done.24 = bf16[3,3072]{1,0:T(4,128)(2,1)S(1)} collective-permute-done((bf16[3,3072]{1,0:T(4,128)(2,1)S(1)}, bf16[3,3072]{1,0:T(4,128)(2,1)S(1)}, u32[]{:S(2)}, u32[]{:S(2)}) %collective-permute-start.24) | collective-permute-done | bytes 18464 | tf_op jit(solution)/shard_map/owners/ppermute | solution.py:449
  (134 shorter events, 26.5 us)
Async XLA Ops:
  0.6 16.6 %copy-start.1 = (bf16[1,128,768]{2,1,0:T(8,128)(2,1)S(1)}, bf16[1,128,768]{2,1,0:T(8,128)(2,1)}, u32[]{:S(2)}) copy-start(bf16[1,128,768]{2,1,0:T(8,128)(2,1)} %param.5) | copy-start | bytes 589828
  0.6 16.6 %copy-start.13 = (bf16[1,128,768]{2,1,0:T(8,128)(2,1)S(1)}, bf16[1,128,768]{2,1,0:T(8,128)(2,1)}, u32[]{:S(2)}) copy-start(bf16[1,128,768]{2,1,0:T(8,128)(2,1)} %param.9) | copy-start | bytes 589828
  0.7 16.6 %collective-permute-start = (bf16[128,768]{1,0:T(8,128)(2,1)}, bf16[128,768]{1,0:T(8,128)(2,1)S(1)}, u32[]{:S(2)}, u32[]{:S(2)}) collective-permute-start(bf16[128,768]{1,0:T(8,128)(2,1)} %bitcast.65), channel_id=1, source_target_pairs={{0,32},{32,0},{1,33},{33,1},{2,34},{34,2},{3,35},{35,3},{4,36},{36... | collective-permute-start | bytes 589832 | tf_op jit(solution)/shard_map/rows_in/ppermute | solution.py:384
  10.4 23.7 %all-to-all-start = ((bf16[32,2,4,1024]{3,2,1,0:T(4,128)(2,1)}), bf16[32,2,4,1024]{3,2,1,0:T(4,128)(2,1)S(1)}, u32[]{:S(2)}, u32[]{:S(2)}) async-start(bf16[32,2,4,1024]{3,2,1,0:T(4,128)(2,1)} %bitcast.8), calls=%async_computation | async-start | bytes 1048576 | tf_op jit(solution)/shard_map/bias_in/all_to_all | solution.py:343
  17.3 10.4 %collective-permute-start.1 = (bf16[3,128,768]{2,1,0:T(8,128)(2,1)S(1)}, bf16[3,128,768]{2,1,0:T(8,128)(2,1)S(1)}, u32[]{:S(2)}, u32[]{:S(2)}) collective-permute-start(bf16[3,128,768]{2,1,0:T(8,128)(2,1)S(1)} %pad_maximum_fusion.refs_0_.refs_4_), channel_id=1, source_target_pairs={{0,1},{1,0},{2,3},{3,2},{4,5},{5,4},{6,7},{7,6},{8,9},{9,8},{10,11... | collective-permute-start | bytes 1769480 | tf_op jit(solution)/shard_map/rows_in/ppermute | solution.py:387
  18.3 21.1 %collective-permute-start.3 = (bf16[3,128,768]{2,1,0:T(8,128)(2,1)S(1)}, bf16[3,128,768]{2,1,0:T(8,128)(2,1)S(1)}, u32[]{:S(2)}, u32[]{:S(2)}) collective-permute-start(bf16[3,128,768]{2,1,0:T(8,128)(2,1)S(1)} %pad_maximum_fusion.refs_0_.refs_4_), channel_id=1, source_target_pairs={{0,128},{64,192},{128,0},{192,64},{1,129},{65,193},{129,1},{193,65... | collective-permute-start | bytes 1769480 | tf_op jit(solution)/shard_map/rows_in/ppermute | solution.py:352
  25.0 27.3 %collective-permute-start.7 = (bf16[3,128,768]{2,1,0:T(8,128)(2,1)S(1)}, bf16[3,128,768]{2,1,0:T(8,128)(2,1)S(1)}, u32[]{:S(2)}, u32[]{:S(2)}) collective-permute-start(bf16[3,128,768]{2,1,0:T(8,128)(2,1)S(1)} %pad_maximum_fusion.refs_0_.refs_4_), channel_id=1, source_target_pairs={{0,64},{64,128},{128,192},{192,0},{1,65},{65,129},{129,193},{193,1... | collective-permute-start | bytes 1769480 | tf_op jit(solution)/shard_map/rows_in/ppermute | solution.py:352
  25.4 27.4 %collective-permute-start.2 = (bf16[3,128,768]{2,1,0:T(8,128)(2,1)S(1)}, bf16[3,128,768]{2,1,0:T(8,128)(2,1)}, u32[]{:S(2)}, u32[]{:S(2)}) collective-permute-start(bf16[3,128,768]{2,1,0:T(8,128)(2,1)S(1)} %pad_maximum_fusion.refs_0_.refs_4_), channel_id=1, source_target_pairs={{0,192},{64,0},{128,64},{192,128},{1,193},{65,1},{129,65},{193,129... | collective-permute-start | bytes 1769480 | tf_op jit(solution)/shard_map/rows_in/ppermute | solution.py:352
  36.3 29.4 %copy-start.11 = (bf16[4,32,1024]{2,1,0:T(8,128)(2,1)}, bf16[4,32,1024]{2,1,0:T(8,128)(2,1)S(1)}, u32[]{:S(2)}) copy-start(bf16[4,32,1024]{2,1,0:T(8,128)(2,1)S(1)} %squeeze.28.refs_5_) | copy-start | bytes 786436
  36.3 16.6 %collective-permute-start.4 = (bf16[4,32,1024]{2,1,0:T(8,128)(2,1)S(1)}, bf16[4,32,1024]{2,1,0:T(8,128)(2,1)S(1)}, u32[]{:S(2)}, u32[]{:S(2)}) collective-permute-start(bf16[4,32,1024]{2,1,0:T(8,128)(2,1)S(1)} %squeeze.28.refs_5_), channel_id=1, source_target_pairs={{0,24},{8,0},{16,8},{24,16},{1,25},{9,1},{17,9},{25,17},{2,26},{10... | collective-permute-start | bytes 786440 | tf_op jit(solution)/shard_map/bias_in/ppermute | solution.py:352
  39.1 13.8 %collective-permute-start.5 = (bf16[4,32,1024]{2,1,0:T(8,128)(2,1)S(1)}, bf16[4,32,1024]{2,1,0:T(8,128)(2,1)S(1)}, u32[]{:S(2)}, u32[]{:S(2)}) collective-permute-start(bf16[4,32,1024]{2,1,0:T(8,128)(2,1)S(1)} %squeeze.28.refs_5_), channel_id=1, source_target_pairs={{0,16},{8,24},{16,0},{24,8},{1,17},{9,25},{17,1},{25,9},{2,18},{10... | collective-permute-start | bytes 786440 | tf_op jit(solution)/shard_map/bias_in/ppermute | solution.py:352
  39.5 15.0 %collective-permute-start.6 = (bf16[4,32,1024]{2,1,0:T(8,128)(2,1)S(1)}, bf16[4,32,1024]{2,1,0:T(8,128)(2,1)S(1)}, u32[]{:S(2)}, u32[]{:S(2)}) collective-permute-start(bf16[4,32,1024]{2,1,0:T(8,128)(2,1)S(1)} %squeeze.28.refs_5_), channel_id=1, source_target_pairs={{0,8},{8,16},{16,24},{24,0},{1,9},{9,17},{17,25},{25,1},{2,10},{10... | collective-permute-start | bytes 786440 | tf_op jit(solution)/shard_map/bias_in/ppermute | solution.py:352
  52.3 6.1 %collective-permute-start.10 = (bf16[3,128,768]{2,1,0:T(8,128)(2,1)S(1)}, bf16[3,128,768]{2,1,0:T(8,128)(2,1)}, u32[]{:S(2)}, u32[]{:S(2)}) collective-permute-start(bf16[3,128,768]{2,1,0:T(8,128)(2,1)S(1)} %collective-permute-done.7.refs_2_.refs_7_), channel_id=1, source_target_pairs={{0,1},{1,0},{2,3},{3,2},{4,5},{5,4},{6,7},{7,6},{8,9},{9,8},{10,11... | collective-permute-start | bytes 1769480 | tf_op jit(solution)/shard_map/project/ppermute | solution.py:401
  52.8 6.4 %collective-permute-start.8 = (bf16[3,128,768]{2,1,0:T(8,128)(2,1)}, bf16[3,128,768]{2,1,0:T(8,128)(2,1)}, u32[]{:S(2)}, u32[]{:S(2)}) collective-permute-start(bf16[3,128,768]{2,1,0:T(8,128)(2,1)} %collective-permute-done.2.refs_0_.refs_5_), channel_id=1, source_target_pairs={{0,1},{1,0},{2,3},{3,2},{4,5},{5,4},{6,7},{7,6},{8,9},{9,8},{10,11... | collective-permute-start | bytes 1769480 | tf_op jit(solution)/shard_map/project/ppermute | solution.py:401
  55.2 4.0 %collective-permute-start.9 = (bf16[3,128,768]{2,1,0:T(8,128)(2,1)}, bf16[3,128,768]{2,1,0:T(8,128)(2,1)S(1)}, u32[]{:S(2)}, u32[]{:S(2)}) collective-permute-start(bf16[3,128,768]{2,1,0:T(8,128)(2,1)} %gate.3.refs_1_.refs_6_), channel_id=1, source_target_pairs={{0,1},{1,0},{2,3},{3,2},{4,5},{5,4},{6,7},{7,6},{8,9},{9,8},{10,11... | collective-permute-start | bytes 1769480 | tf_op jit(solution)/shard_map/project/ppermute | solution.py:401
  56.2 21.5 %collective-permute-start.11 = (bf16[4,32,1024]{2,1,0:T(8,128)(2,1)S(1)}, bf16[4,32,1024]{2,1,0:T(8,128)(2,1)S(1)}, u32[]{:S(2)}, u32[]{:S(2)}) collective-permute-start(bf16[4,32,1024]{2,1,0:T(8,128)(2,1)S(1)} %squeeze.29.refs_5_), channel_id=1, source_target_pairs={{0,24},{8,0},{16,8},{24,16},{1,25},{9,1},{17,9},{25,17},{2,26},{10... | collective-permute-start | bytes 786440 | tf_op jit(solution)/shard_map/bias_in/ppermute | solution.py:352
  58.1 20.6 %collective-permute-start.12 = (bf16[4,32,1024]{2,1,0:T(8,128)(2,1)S(1)}, bf16[4,32,1024]{2,1,0:T(8,128)(2,1)S(1)}, u32[]{:S(2)}, u32[]{:S(2)}) collective-permute-start(bf16[4,32,1024]{2,1,0:T(8,128)(2,1)S(1)} %squeeze.29.refs_5_), channel_id=1, source_target_pairs={{0,16},{8,24},{16,0},{24,8},{1,17},{9,25},{17,1},{25,9},{2,18},{10... | collective-permute-start | bytes 786440 | tf_op jit(solution)/shard_map/bias_in/ppermute | solution.py:352
  58.5 20.2 %collective-permute-start.13 = (bf16[4,32,1024]{2,1,0:T(8,128)(2,1)S(1)}, bf16[4,32,1024]{2,1,0:T(8,128)(2,1)S(1)}, u32[]{:S(2)}, u32[]{:S(2)}) collective-permute-start(bf16[4,32,1024]{2,1,0:T(8,128)(2,1)S(1)} %squeeze.29.refs_5_), channel_id=1, source_target_pairs={{0,8},{8,16},{16,24},{24,0},{1,9},{9,17},{17,25},{25,1},{2,10},{10... | collective-permute-start | bytes 786440 | tf_op jit(solution)/shard_map/bias_in/ppermute | solution.py:352
  74.4 21.5 %collective-permute-start.15 = (bf16[4,32,1024]{2,1,0:T(8,128)(2,1)}, bf16[4,32,1024]{2,1,0:T(8,128)(2,1)S(1)}, u32[]{:S(2)}, u32[]{:S(2)}) collective-permute-start(bf16[4,32,1024]{2,1,0:T(8,128)(2,1)} %get-tuple-element.37), channel_id=1, source_target_pairs={{0,8},{8,16},{16,24},{24,0},{1,9},{9,17},{17,25},{25,1},{2,10},{10... | collective-permute-start | bytes 786440 | tf_op jit(solution)/shard_map/along_y/ppermute | solution.py:357
  76.1 26.2 %collective-permute-start.16 = (bf16[4,32,1024]{2,1,0:T(8,128)(2,1)}, bf16[4,32,1024]{2,1,0:T(8,128)(2,1)S(1)}, u32[]{:S(2)}, u32[]{:S(2)}) collective-permute-start(bf16[4,32,1024]{2,1,0:T(8,128)(2,1)} %get-tuple-element.38), channel_id=1, source_target_pairs={{0,16},{8,24},{16,0},{24,8},{1,17},{9,25},{17,1},{25,9},{2,18},{10... | collective-permute-start | bytes 786440 | tf_op jit(solution)/shard_map/along_y/ppermute | solution.py:357
  77.6 24.7 %collective-permute-start.17 = (bf16[4,32,1024]{2,1,0:T(8,128)(2,1)}, bf16[4,32,1024]{2,1,0:T(8,128)(2,1)S(1)}, u32[]{:S(2)}, u32[]{:S(2)}) collective-permute-start(bf16[4,32,1024]{2,1,0:T(8,128)(2,1)} %get-tuple-element.39), channel_id=1, source_target_pairs={{0,24},{8,0},{16,8},{24,16},{1,25},{9,1},{17,9},{25,17},{2,26},{10... | collective-permute-start | bytes 786440 | tf_op jit(solution)/shard_map/along_y/ppermute | solution.py:357
  88.2 17.7 %collective-permute-start.18 = (bf16[4,32,1024]{2,1,0:T(8,128)(2,1)}, bf16[4,32,1024]{2,1,0:T(8,128)(2,1)S(1)}, u32[]{:S(2)}, u32[]{:S(2)}) collective-permute-start(bf16[4,32,1024]{2,1,0:T(8,128)(2,1)} %get-tuple-element.41), channel_id=1, source_target_pairs={{0,8},{8,16},{16,24},{24,0},{1,9},{9,17},{17,25},{25,1},{2,10},{10... | collective-permute-start | bytes 786440 | tf_op jit(solution)/shard_map/along_y/ppermute | solution.py:357
  88.7 19.1 %collective-permute-start.19 = (bf16[4,32,1024]{2,1,0:T(8,128)(2,1)}, bf16[4,32,1024]{2,1,0:T(8,128)(2,1)S(1)}, u32[]{:S(2)}, u32[]{:S(2)}) collective-permute-start(bf16[4,32,1024]{2,1,0:T(8,128)(2,1)} %get-tuple-element.42), channel_id=1, source_target_pairs={{0,16},{8,24},{16,0},{24,8},{1,17},{9,25},{17,1},{25,9},{2,18},{10... | collective-permute-start | bytes 786440 | tf_op jit(solution)/shard_map/along_y/ppermute | solution.py:357
  90.1 28.5 %all-to-all-start.1 = ((bf16[8,576,128]{2,1,0:T(8,128)(2,1)}), bf16[8,576,128]{2,1,0:T(8,128)(2,1)S(1)}, u32[]{:S(2)}, u32[]{:S(2)}) async-start(bf16[8,576,128]{2,1,0:T(8,128)(2,1)} %bitcast.68), calls=%async_computation.1 | async-start | bytes 2359296 | tf_op jit(solution)/shard_map/tokens_out/all_to_all | solution.py:343
  95.9 11.9 %collective-permute-start.20 = (bf16[4,32,1024]{2,1,0:T(8,128)(2,1)}, bf16[4,32,1024]{2,1,0:T(8,128)(2,1)}, u32[]{:S(2)}, u32[]{:S(2)}) collective-permute-start(bf16[4,32,1024]{2,1,0:T(8,128)(2,1)} %get-tuple-element.43), channel_id=1, source_target_pairs={{0,24},{8,0},{16,8},{24,16},{1,25},{9,1},{17,9},{25,17},{2,26},{10... | collective-permute-start | bytes 786440 | tf_op jit(solution)/shard_map/along_y/ppermute | solution.py:357
  103.6 7.8 %collective-permute-start.21 = (bf16[240,384]{1,0:T(8,128)(2,1)}, bf16[240,384]{1,0:T(8,128)(2,1)S(1)}, u32[]{:S(2)}, u32[]{:S(2)}) collective-permute-start(bf16[240,384]{1,0:T(8,128)(2,1)} %get-tuple-element.49), channel_id=1, source_target_pairs={{0,8},{8,16},{16,24},{24,0},{1,9},{9,17},{17,25},{25,1},{2,10},{10... | collective-permute-start | bytes 552968 | tf_op jit(solution)/shard_map/along_y/ppermute | solution.py:357
  104.4 10.1 %collective-permute-start.22 = (bf16[240,384]{1,0:T(8,128)(2,1)}, bf16[240,384]{1,0:T(8,128)(2,1)}, u32[]{:S(2)}, u32[]{:S(2)}) collective-permute-start(bf16[240,384]{1,0:T(8,128)(2,1)} %get-tuple-element.50), channel_id=1, source_target_pairs={{0,16},{8,24},{16,0},{24,8},{1,17},{9,25},{17,1},{25,9},{2,18},{10... | collective-permute-start | bytes 552968 | tf_op jit(solution)/shard_map/along_y/ppermute | solution.py:357
  105.9 9.4 %collective-permute-start.23 = (bf16[240,384]{1,0:T(8,128)(2,1)}, bf16[240,384]{1,0:T(8,128)(2,1)}, u32[]{:S(2)}, u32[]{:S(2)}) collective-permute-start(bf16[240,384]{1,0:T(8,128)(2,1)} %get-tuple-element.51), channel_id=1, source_target_pairs={{0,24},{8,0},{16,8},{24,16},{1,25},{9,1},{17,9},{25,17},{2,26},{10... | collective-permute-start | bytes 552968 | tf_op jit(solution)/shard_map/along_y/ppermute | solution.py:357
  118.7 41.0 %all-to-all-start.2 = ((bf16[32,8,1600]{2,1,0:T(8,128)(2,1)}), bf16[32,8,1600]{2,1,0:T(8,128)(2,1)S(1)}, u32[]{:S(2)}, u32[]{:S(2)}) async-start(bf16[32,8,1600]{2,1,0:T(8,128)(2,1)} %maximum_maximum_fusion), calls=%async_computation.2 | async-start | bytes 1703936 | tf_op jit(solution)/shard_map/owners/all_to_all | solution.py:343
  127.7 26.2 %copy-start.15 = (bf16[768,2304]{1,0:T(8,128)(2,1)S(1)}, bf16[768,2304]{1,0:T(8,128)(2,1)}, u32[]{:S(2)}) copy-start(bf16[768,2304]{1,0:T(8,128)(2,1)} %w_qkv.1) | copy-start | bytes 10616836
  130.5 23.4 %collective-permute-start.14 = (bf16[128,768]{1,0:T(8,128)(2,1)S(1)}, bf16[128,768]{1,0:T(8,128)(2,1)S(1)}, u32[]{:S(2)}, u32[]{:S(2)}) collective-permute-start(bf16[128,768]{1,0:T(8,128)(2,1)S(1)} %fusion.2), channel_id=1, source_target_pairs={{0,32},{32,0},{1,33},{33,1},{2,34},{34,2},{3,35},{35,3},{4,36},{36... | collective-permute-start | bytes 589832 | tf_op jit(solution)/shard_map/tokens_out/ppermute | solution.py:465
  161.1 6.7 %collective-permute-start.24 = (bf16[3,3072]{1,0:T(4,128)(2,1)S(1)}, bf16[3,3072]{1,0:T(4,128)(2,1)S(1)}, u32[]{:S(2)}, u32[]{:S(2)}) collective-permute-start(bf16[3,3072]{1,0:T(4,128)(2,1)S(1)} %bitcast.77), channel_id=1, source_target_pairs={{0,32},{32,0},{1,33},{33,1},{2,34},{34,2},{3,35},{35,3},{4,36},{36... | collective-permute-start | bytes 55304 | tf_op jit(solution)/shard_map/owners/ppermute | solution.py:449
  (18 other events, 78.2 us)
